TPU v7x, 32 devices: a whole 2x2x4 slice. The times are simulated.
32 devices in a mesh: rows: 8 (over z, x), tp: 4 (over y, core).
Axes of the slice: x: 2, y: 2, z: 4, core: 2. Of those that a mesh axis runs over, the one named last changes fastest.
Arguments:
- tokens: bfloat16 [1024, 8, 1024], P('tp', 'rows'), may hold values from -6 to 6
- memory: bfloat16 [1024, 8, 1024], P('tp', 'rows'), may hold values from -6 to 6
- out_grad: bfloat16 [1024, 8, 1024], P('tp', 'rows'), may hold values from -6 to 6
- dec_segments: int32 [8, 1024], P('rows'), may hold values from 0 to 2, as said below
- src_segments: int32 [8, 1024], P('rows'), may hold values from 0 to 2, as said below
- self_query: bfloat16 [1024, 1024], P(None, 'tp'), may hold values from -0.1875 to 0.1875
- self_key: bfloat16 [1024, 1024], P(None, 'tp'), may hold values from -0.1875 to 0.1875
- self_value: bfloat16 [1024, 1024], P(None, 'tp'), may hold values from -0.1875 to 0.1875
- self_out: bfloat16 [1024, 1024], P('tp'), may hold values from -1.5 to 1.5
- cross_query: bfloat16 [1024, 1024], P(None, 'tp'), may hold values from -0.1875 to 0.1875
- cross_key: bfloat16 [1024, 1024], P(None, 'tp'), may hold values from -0.1875 to 0.1875
- cross_value: bfloat16 [1024, 1024], P(None, 'tp'), may hold values from -0.1875 to 0.1875
- cross_out: bfloat16 [1024, 1024], P('tp'), may hold values from -1.5 to 1.5
- ffn_in: bfloat16 [1024, 4096], P(None, 'tp'), may hold values from -0.1875 to 0.1875
- ffn_out: bfloat16 [4096, 1024], P('tp'), may hold values from -0.09375 to 0.09375
- adapt_down: bfloat16 [1024, 512], replicated, may hold values from -0.1875 to 0.1875
- adapt_down_bias: float32 [512], replicated, may hold values from -3 to 3
- adapt_up: bfloat16 [512, 1024], replicated, may hold values from -0.0625 to 0.0625
- adapt_up_bias: float32 [1024], replicated, may hold values from -0.6 to 0.6
- self_prefix: bfloat16 [2, 30, 1024], P(None, None, 'tp'), may hold values from -6 to 6
- cross_prefix: bfloat16 [2, 30, 1024], P(None, None, 'tp'), may hold values from -6 to 6
- norm_gain: float32 [3, 1024], replicated, may hold values from 0.5 to 1.5
- norm_shift: float32 [3, 1024], replicated, may hold values from -1.8 to 1.8
Outputs:
- output: bfloat16 [1024, 8, 1024], P('tp', 'rows')
- tokens_grad: bfloat16 [1024, 8, 1024], P('tp', 'rows')
- memory_grad: bfloat16 [1024, 8, 1024], P('tp', 'rows')
- self_prefix_grad: float32 [2, 30, 1024], P(None, None, 'tp')
- cross_prefix_grad: float32 [2, 30, 1024], P(None, None, 'tp')
- gain_grad: float32 [3, 1024], replicated
- shift_grad: float32 [3, 1024], replicated
- adapt_down_grad: float32 [1024, 512], replicated
- adapt_down_bias_grad: float32 [512], replicated
- adapt_up_grad: float32 [512, 1024], replicated
- adapt_up_bias_grad: float32 [1024], replicated
Inputs may be any that keep to these rules, and one draw needn't show every extreme that they name: `dec_segments`: each row holds documents 0, 1 and 2 in this order; document 1 begins at a position from 1 to 127 and ends among the last 128 positions, before the row's last position. `src_segments`: each row holds documents 0, 1 and 2 in this order; document 1 begins at a position from 1 to 127 and ends among the last 128 positions, before the row's last position.
All inputs are finite; a program needn't handle non-finite values.
Results may differ from a plain program's by a relative error of at most 0.025.
Values may be sent and summed in bfloat16 or wider, within the bound.
A program may use at most 192 MiB of HBM per device.

v0:
```python
import functools

import jax
import jax.numpy as jnp
from jax import lax
from jax.experimental import pallas as pl
from jax.experimental.pallas import tpu as pltpu
from jax.sharding import PartitionSpec as P

HEAD = 64
PAIR = 2 * HEAD
PRE = 128
PRE_PACK = 32
GROUP = 8
LINE = 4
MASKED = -1000000000.0
EPSILON = 1e-05
SCALE = HEAD**-0.5
f32 = jnp.float32
bf16 = jnp.bfloat16
MESH = pl.DeviceIdType.MESH
VMEM = pltpu.VMEM
ANY = pl.ANY


def nn(a, b):
    return lax.dot_general(a, b, (((1,), (0,)), ((), ())), preferred_element_type=f32)


def nt(a, b):
    return lax.dot_general(a, b, (((1,), (1,)), ((), ())), preferred_element_type=f32)


def tn(a, b):
    return lax.dot_general(a, b, (((0,), (0,)), ((), ())), preferred_element_type=f32)


def gelu_parts(v):
    phi = 0.5 + 0.5 * lax.erf(v * (0.5**0.5))
    slope = phi + v * (jnp.exp(-0.5 * v * v) * 0.3989422804014327)
    return v * phi, slope


def norm_parts(v):
    centered = v - jnp.mean(v, axis=-1, keepdims=True)
    spread = lax.rsqrt(jnp.mean(centered * centered, axis=-1, keepdims=True) + EPSILON)
    return centered * spread, spread


def norm_back(dy, gain, n, spread):
    dn = dy * gain
    dv = spread * (
        dn - jnp.mean(dn, axis=-1, keepdims=True) - n * jnp.mean(dn * n, axis=-1, keepdims=True)
    )
    return dv, jnp.sum(dy * n, axis=0, keepdims=True), jnp.sum(dy, axis=0, keepdims=True)


def lane_half(shape, h):
    return (lax.broadcasted_iota(jnp.int32, shape, 1) // HEAD) == h


def mask_bias(seg_q, seg_k, q_index, k_index, prefix_len):
    keep = seg_q == seg_k
    if q_index is not None:
        keep = keep & (k_index - PRE <= q_index)
    keep = keep | (k_index < prefix_len)
    return jnp.where(keep, 0.0, MASKED)


def pair_forward(q_pair, k_pair, v_pair, bias):
    outs, logs = [], []
    for h in range(2):
        half = lane_half(q_pair.shape, h)
        scores = nt(jnp.where(half, q_pair, jnp.zeros_like(q_pair)), k_pair) + bias
        top = jnp.max(scores, axis=1, keepdims=True)
        e = jnp.exp(scores - top)
        total = jnp.sum(e, axis=1, keepdims=True)
        outs.append(nn(e.astype(bf16), v_pair) * (1.0 / total))
        logs.append(top + jnp.log(total))
    return jnp.where(lane_half(outs[0].shape, 0), outs[0], outs[1]).astype(bf16), logs


def keep_logs(kept, logs, j):
    lane = lax.broadcasted_iota(jnp.int32, kept.shape, 1)
    for h in range(2):
        kept[...] = jnp.where(lane == 2 * j + h, logs[h], kept[...])


def pair_backward(q_pair, k_pair, v_pair, a_pair, da_pair, logs, bias_t):
    k_turned = k_pair.T
    prod = da_pair.astype(f32) * a_pair.astype(f32)
    prod_high = prod.astype(bf16)
    prod_low = (prod - prod_high.astype(f32)).astype(bf16)
    pick = (
        lax.broadcasted_iota(jnp.int32, (8, PAIR), 1) // HEAD
        == lax.broadcasted_iota(jnp.int32, (8, PAIR), 0)
    ).astype(bf16)
    delta = nt(pick, prod_high) + nt(pick, prod_low)
    dk = dv = None
    dq = []
    for h in range(2):
        half = lane_half(q_pair.shape, h)
        q = jnp.where(half, q_pair, jnp.zeros_like(q_pair))
        da = jnp.where(half, da_pair, jnp.zeros_like(da_pair))
        p = jnp.exp(nt(k_pair, q) + (bias_t - logs[h]))
        ds = (p * (nt(v_pair, da) - delta[h : h + 1])).astype(bf16)
        dv_h = nn(p.astype(bf16), da)
        dk_h = nn(ds, q)
        dk = dk_h if dk is None else dk + dk_h
        dv = dv_h if dv is None else dv + dv_h
        dq.append(nn(k_turned[h * HEAD : (h + 1) * HEAD], ds))
    return jnp.concatenate(dq, axis=0).T.astype(bf16), dk, dv


def cross_forward_kernel(
    prefix_len, v1, memory, wq, wk, wv, wo, pre, seg_col, seg_row, gain, shift, own,
    q_out, k_out, v_out, a_out, l_out, v2, full, n1_low, bias, kept, stage, send, recv, local,
):
    step = pl.program_id(0)
    block, lanes = q_out.shape[1:]
    keys = k_out.shape[1]
    links = Links(send, recv)
    weights = WeightGather(links, 0, 2, [own], [full], [stage], local)

    @pl.when(step == 0)
    def _():
        greet(
            [links.tp_peer(1), links.tp_peer(2)]
            + [links.line_peer(d) for d in range(1, LINE)]
            + [links.side_peer()]
        )
        weights.start_over(0)
        weights.start_beside(0)

    @pl.when(step == 0)
    def _():
        n, _ = norm_parts(v1[...])
        normed = n * gain[0:1] + shift[0:1]
        v2[...] = normed
        n1_low[...] = normed.astype(bf16)
        kept[...] = jnp.zeros_like(kept)
        bias[...] = mask_bias(
            seg_col[...],
            seg_row[...],
            None,
            lax.broadcasted_iota(jnp.int32, (block, keys), 1),
            prefix_len,
        )

    q_out[0] = (SCALE * nn(n1_low[...], wq[0])).astype(bf16)
    for target, at in ((k_out, 0), (v_out, PRE_PACK)):
        target[0, 0:PRE_PACK] = pre[0, at : at + PRE_PACK]
        target[0, PRE_PACK:PRE] = jnp.zeros((PRE - PRE_PACK, lanes), bf16)

    @pl.loop(0, (keys - PRE) // block)
    def _(i):
        at = pl.multiple_of(i * block, block)
        rows = memory[pl.ds(at, block)]
        k_out[0, pl.ds(PRE + at, block)] = nn(rows, wk[0]).astype(bf16)
        v_out[0, pl.ds(PRE + at, block)] = nn(rows, wv[0]).astype(bf16)

    @pl.loop(0, lanes // PAIR)
    def _(j):
        cols = pl.ds(pl.multiple_of(j * PAIR, PAIR), PAIR)
        mixture, logs = pair_forward(
            q_out[0, :, cols], k_out[0, :, cols], v_out[0, :, cols], bias[...]
        )
        a_out[0, :, cols] = mixture
        keep_logs(kept, logs, j)

    l_out[0] = kept[...].T[0:8]
    v2[...] += nn(a_out[0], wo[0])

    @pl.when(step == 0)
    def _():
        weights.keep_own(0)
        weights.came_over(0)

    @pl.when(step == 1)
    def _():
        weights.along(0, 0)

    @pl.when(step == 2)
    def _():
        weights.along(0, 1)

    @pl.when(step == pl.num_programs(0) - 1)
    def _():
        weights.along(0, 2)
        weights.complete(0)
        weights.finish(0)


def whole_spec(shape):
    return pl.BlockSpec(shape, lambda i: (0,) * len(shape))


def shard_spec(shape, index=lambda i: i):
    return pl.BlockSpec((1,) + shape[1:], lambda i: (index(i), 0, 0))


def cross_forward(prefix_len, v1, memory, weights, pre, seg_col, seg_row, gain, shift, own):
    wq, wk, wv, wo = weights
    n, width, lanes = wq.shape
    block = v1.shape[0]
    seq = memory.shape[0]
    out = jax.ShapeDtypeStruct
    outs = (
        out((n, block, lanes), bf16),
        out((n, PRE + seq, lanes), bf16),
        out((n, PRE + seq, lanes), bf16),
        out((n, block, lanes), bf16),
        out((n, 8, block), f32),
    )
    return pl.pallas_call(
        functools.partial(cross_forward_kernel, prefix_len),
        grid=(n,),
        out_shape=outs + (out((block, width), f32), out((n,) + own.shape, own.dtype)),
        in_specs=[whole_spec(v1.shape), whole_spec(memory.shape)]
        + [shard_spec(a.shape) for a in (wq, wk, wv, wo, pre)]
        + [whole_spec(a.shape) for a in (seg_col, seg_row, gain, shift)]
        + [pl.BlockSpec(memory_space=pltpu.HBM)],
        out_specs=[shard_spec(a.shape) for a in outs]
        + [whole_spec((block, width)), pl.BlockSpec(memory_space=pltpu.HBM)],
        scratch_shapes=[
            VMEM((block, width), bf16),
            VMEM((block, PRE + seq), f32),
            VMEM((block, 128), f32),
            VMEM(own.shape, own.dtype),
            pltpu.SemaphoreType.DMA((FLOWS,)),
            pltpu.SemaphoreType.DMA((FLOWS,)),
            pltpu.SemaphoreType.DMA((2,)),
        ],
        compiler_params=pltpu.CompilerParams(
            collective_id=1, has_side_effects=True, vmem_limit_bytes=48 << 20
        ),
        name="cross_forward",
    )(v1, memory, wq, wk, wv, wo, pre, seg_col, seg_row, gain, shift, own)


def feed_forward_kernel(
    v2, out_grad, w_in, w_out, down, down_bias, up, up_bias, gain, shift,
    output, dr2, grads, vecs,
    n2_low, n2_hat, total, e_low, slope, grad,
):
    step = pl.program_id(0)
    half = pl.num_programs(0) // 2
    width = v2.shape[1]

    @pl.when(step == 0)
    def _():
        n, _ = norm_parts(v2[...])
        n2_hat[...] = n
        normed = n * gain[1:2] + shift[1:2]
        total[...] = normed
        n2_low[...] = normed.astype(bf16)

    @pl.when(step < half)
    def _():
        act, bend = gelu_parts(nn(n2_low[...], w_in[0]))
        slope[step] = bend
        total[...] += nn(act.astype(bf16), w_out[0])

    @pl.when(step == half - 1)
    def _():
        act, bend = gelu_parts(nn(n2_low[...], down[...]) + down_bias[...])
        act = act.astype(bf16)
        resid = total[...] + 4.0 * (nn(act, up[...]) + up_bias[...])
        n, spread = norm_parts(resid)
        output[...] = (n * gain[2:3] + shift[2:3]).astype(bf16)
        dz, gain_part, shift_part = norm_back(out_grad[...].astype(f32), gain[2:3], n, spread)
        e_low[...] = dz.astype(bf16)
        four = (4.0 * dz).astype(bf16)
        grads[0] = tn(act, four).astype(bf16)
        da = (nt(four, up[...]) * bend).astype(bf16)
        grads[1] = tn(da, n2_low[...]).astype(bf16)
        grad[...] = dz + nt(da, down[...])
        vecs[...] = jnp.zeros_like(vecs)
        vecs[2:3] = gain_part
        vecs[5:6] = shift_part
        vecs[6:7] = jnp.sum(four.astype(f32), axis=0, keepdims=True)
        vecs[7:8, 0 : down.shape[1]] = jnp.sum(da.astype(f32), axis=0, keepdims=True)

    @pl.when(step >= half)
    def _():
        du = (nt(e_low[...], w_out[0]) * slope[2 * half - 1 - step]).astype(bf16)
        grad[...] += nt(du, w_in[0])

    @pl.when(step == 2 * half - 1)
    def _():
        _, spread = norm_parts(v2[...])
        dv, gain_part, shift_part = norm_back(grad[...], gain[1:2], n2_hat[...], spread)
        dr2[...] = dv
        vecs[1:2] = gain_part
        vecs[4:5] = shift_part


def feed_forward(v2, out_grad, w_in, w_out, down, down_bias, up, up_bias, gain, shift):
    n, width, inner = w_in.shape
    block = v2.shape[0]
    adapt = down.shape[1]
    out = jax.ShapeDtypeStruct
    outs = (
        out((block, width), bf16),
        out((block, width), f32),
        out((2, adapt, width), bf16),
        out((8, width), f32),
    )
    turn = lambda i: jnp.minimum(i, 2 * n - 1 - i)
    return pl.pallas_call(
        feed_forward_kernel,
        grid=(2 * n,),
        out_shape=outs,
        in_specs=[whole_spec(v2.shape), whole_spec(out_grad.shape)]
        + [shard_spec(w_in.shape, turn), shard_spec(w_out.shape, turn)]
        + [whole_spec(a.shape) for a in (down, down_bias, up, up_bias, gain, shift)],
        out_specs=[whole_spec(a.shape) for a in outs],
        scratch_shapes=[
            VMEM((block, width), bf16),
            VMEM((block, width), f32),
            VMEM((block, width), f32),
            VMEM((block, width), bf16),
            VMEM((n, block, inner), f32),
            VMEM((block, width), f32),
        ],
        compiler_params=pltpu.CompilerParams(vmem_limit_bytes=56 << 20),
        name="feed_forward",
    )(v2, out_grad, w_in, w_out, down, down_bias, up, up_bias, gain, shift)


class Links:
    def __init__(self, send, recv):
        self.send, self.recv = send, recv
        self.row = lax.axis_index("rows")
        self.t = lax.axis_index("tp")
        self.flows = 0
        place = lax.rem(self.row, GROUP)
        self.base = self.row - place
        self.a = place // 2
        self.b = lax.rem(place, 2)
        self.place = place

    def flow(self):
        self.flows += 1
        return self.flows - 1

    def tp_peer(self, mask):
        return (self.row, self.t ^ mask)

    def line_peer(self, d):
        return (self.base + lax.rem(self.a + d, LINE) * 2 + self.b, self.t)

    def side_peer(self):
        return (self.base + self.a * 2 + (1 - self.b), self.t)

    def copy(self, src, dst, flow, peer):
        return pltpu.make_async_remote_copy(
            src_ref=src,
            dst_ref=dst,
            send_sem=self.send.at[flow],
            recv_sem=self.recv.at[flow],
            device_id=peer,
            device_id_type=MESH,
        )

    def start(self, src, dst, flow, peer):
        made = self.copy(src, dst, flow, peer)
        made.start()
        return made

    def arrived(self, dst, flow, peer):
        self.copy(dst, dst, flow, peer).wait_recv()


def greet(peers):
    barrier = pltpu.get_barrier_semaphore()
    for peer in peers:
        pl.semaphore_signal(barrier, inc=1, device_id=peer, device_id_type=MESH)
    pl.semaphore_wait(barrier, len(peers))


CHUNKS = 4


FLOWS = 14


class WeightGather:
    def __init__(self, links, base, across, own, full, stage, local):
        self.links, self.base, self.across = links, base, across
        self.own, self.full, self.stage, self.local = own, full, stage, local
        self.far, self.last = links.t ^ 2, links.t ^ 3
        a = links.a
        self.right = (links.base + jnp.minimum(a + 1, LINE - 1) * 2 + links.b, links.t)
        self.left = (links.base + jnp.maximum(a - 1, 0) * 2 + links.b, links.t)
        self.side = links.side_peer()
        self.sibling = links.tp_peer(1)
        self.over = links.tp_peer(2)

    def at(self, i, a, b):
        rows = self.own[i].shape[0] // GROUP
        return pl.ds(pl.multiple_of((a * 2 + b) * rows, rows), rows)

    def part(self, i, a, b):
        return self.full[i].at[self.far, self.at(i, a, b)]

    def flow(self, i, k):
        return self.base + i * FLOWS + k

    def over_copy(self, i, k):
        links = self.links
        b = links.b if k == 0 else 1 - links.b
        at = self.at(i, links.a, b)
        return links.copy(
            self.own[i].at[at], self.full[i].at[links.t, at], self.flow(i, k), self.over
        )

    def beside_copy(self, i):
        return self.links.copy(
            self.own[i], self.full[i].at[self.links.t], self.flow(i, 2), self.sibling
        )

    def pass_copy(self, i):
        whole = self.full[i].at[self.far]
        return self.links.copy(whole, whole, self.flow(i, 3), self.sibling)

    def moved(self, i, a, flow, peer):
        part = self.part(i, a, self.links.b)
        return self.links.copy(part, part, self.flow(i, flow), peer)

    def stage_in(self, i):
        return pltpu.make_async_copy(self.own[i], self.stage[i], self.local.at[2 * i])

    def stage_out(self, i):
        return pltpu.make_async_copy(
            self.stage[i], self.full[i].at[self.links.t], self.local.at[2 * i + 1]
        )

    def start_over(self, i):
        for k in range(self.across):
            self.over_copy(i, k).start()

    def start_beside(self, i):
        self.beside_copy(i).start()
        self.stage_in(i).start()

    def keep_own(self, i):
        self.stage_in(i).wait()
        self.stage_out(i).start()

    def came_over(self, i):
        mine = self.part(i, self.links.a, self.links.b)
        self.links.arrived(mine, self.flow(i, 0), self.over)
        self.spread(i)

    def spread(self, i):
        a = self.links.a

        @pl.when(a < LINE - 1)
        def _():
            self.moved(i, a, 4, self.right).start()

        @pl.when(a > 0)
        def _():
            self.moved(i, a, 7, self.left).start()

        if self.across == 1:
            self.moved(i, a, 10, self.side).start()

    def along(self, i, k):
        links, a = self.links, self.links.a

        @pl.when(a - 1 - k >= 0)
        def _():
            links.arrived(self.part(i, a - 1 - k, links.b), self.flow(i, 4 + k), self.left)
            if k < LINE - 2:

                @pl.when(a < LINE - 1)
                def _():
                    self.moved(i, a - 1 - k, 5 + k, self.right).start()

            self.moved(i, a - 1 - k, 11 + k, self.side).start()

        @pl.when(a + 1 + k <= LINE - 1)
        def _():
            links.arrived(self.part(i, a + 1 + k, links.b), self.flow(i, 7 + k), self.right)
            if k < LINE - 2:

                @pl.when(a > 0)
                def _():
                    self.moved(i, a + 1 + k, 8 + k, self.left).start()

            self.moved(i, a + 1 + k, 13 - k, self.side).start()

    def side_part(self, i, k):
        links, a = self.links, self.links.a
        if k == 0:
            return self.part(i, a, 1 - links.b)
        piece = jnp.where(k <= a, a - k, a + LINE - k)
        return self.part(i, piece, 1 - links.b)

    def complete(self, i):
        links = self.links
        if self.across == 2:
            links.arrived(self.side_part(i, 0), self.flow(i, 1), self.over)
        for k in range(self.across - 1, LINE):
            links.arrived(self.side_part(i, k), self.flow(i, 10 + k), self.side)
        self.pass_copy(i).start()

    def finish(self, i):
        links = self.links
        links.arrived(self.full[i].at[links.t ^ 1], self.flow(i, 2), self.sibling)
        links.arrived(self.full[i].at[self.last], self.flow(i, 3), self.sibling)
        for k in range(self.across):
            self.over_copy(i, k).wait_send()
        self.beside_copy(i).wait_send()
        self.stage_out(i).wait()
        self.spread_sent(i)

    def spread_sent(self, i):
        a = self.links.a
        self.pass_copy(i).wait_send()
        for k in range(LINE - 1):

            @pl.when((a < LINE - 1) & (a - k >= 0))
            def _():
                self.moved(i, a - k, 4 + k, self.right).wait_send()

            @pl.when((a > 0) & (a + k <= LINE - 1))
            def _():
                self.moved(i, a + k, 7 + k, self.left).wait_send()

        for k in range(self.across - 1, LINE):
            piece = a if k == 0 else jnp.where(k <= a, a - k, a + LINE - k)
            self.moved(i, piece, 10 + k, self.side).wait_send()


class AdapterSpread(WeightGather):
    def __init__(self, links, base, full):
        super().__init__(links, base, 1, None, full, None, None)
        self.half = lax.rem(links.t, 2)

    def part(self, i, a, b):
        return self.full.at[self.half, b, a]

    def pass_copy(self, i):
        whole = self.full.at[self.half]
        return self.links.copy(whole, whole, self.flow(i, 3), self.sibling)

    def finish(self, i):
        self.links.arrived(self.full.at[1 - self.half], self.flow(i, 3), self.sibling)
        self.spread_sent(i)


class AdapterReduce:
    def __init__(self, links, base, levels, g, s1, h, xb, h2, zb, p3, yb, hb):
        self.links, self.base, self.levels = links, base, levels
        self.g, self.s1, self.h, self.xb, self.h2 = g, s1, h, xb, h2
        self.zb, self.p3, self.yb, self.hb = zb, p3, yb, hb
        self.half = lax.rem(links.t, 2)
        self.groups = [(links.row ^ (GROUP << level), links.t) for level in range(levels)]

    def beside(self):
        return self.links.copy(
            self.g.at[1 - self.half], self.s1, self.base, self.links.tp_peer(1)
        )

    def side(self):
        links = self.links
        return links.copy(self.h.at[1 - links.b], self.xb, self.base + 1, links.side_peer())

    def line(self, d):
        links = self.links
        return links.copy(
            self.h2.at[lax.rem(links.a + d, LINE)],
            self.zb.at[d - 1],
            self.base + 1 + d,
            links.line_peer(d),
        )

    def over(self):
        return self.links.copy(self.p3, self.yb, self.base + 1 + LINE, self.links.tp_peer(2))

    def group(self, level):
        return self.links.copy(
            self.hb.at[2 * level],
            self.hb.at[2 * level + 1],
            self.base + 2 + LINE + level,
            self.groups[level],
        )

    def phase(self, number):
        if number == 0:
            self.beside().start()
        elif number == 1:
            self.beside().wait()
            self.h[...] = (self.g[self.half].astype(f32) + self.s1[...].astype(f32)).astype(bf16)
            self.side().start()
        elif number == 2:
            self.side().wait()
            self.h2[...] = (
                self.h[self.links.b].astype(f32) + self.xb[...].astype(f32)
            ).astype(bf16)
            for d in range(1, LINE):
                self.line(d).start()
        elif number == 3:
            for d in range(1, LINE):
                self.line(d).wait()
            total = self.h2[self.links.a].astype(f32)
            for d in range(1, LINE):
                total = total + self.zb[d - 1].astype(f32)
            self.p3[...] = total.astype(bf16)
            self.over().start()

    def result(self):
        self.over().wait()
        value = self.p3[...].astype(f32) + self.yb[...].astype(f32)
        for level in range(self.levels):
            self.hb[2 * level] = value.astype(bf16)
            self.group(level).start()
            self.group(level).wait()
            value = self.hb[2 * level].astype(f32) + self.hb[2 * level + 1].astype(f32)
        return value.astype(bf16)


class RowGather:
    FLOWS = 1 + 2 * 4

    def __init__(self, links, base, own, full):
        self.links, self.base, self.own, self.full = links, base, own, full
        self.far, self.last = links.t ^ 2, links.t ^ 3
        self.sibling, self.over = links.tp_peer(1), links.tp_peer(2)

    def at(self, c):
        rows = self.own.shape[0] // CHUNKS
        return pl.ds(c * rows, rows)

    def beside_copy(self):
        return self.links.copy(self.own, self.full.at[self.links.t], self.base, self.sibling)

    def over_copy(self, c):
        at = self.at(c)
        return self.links.copy(
            self.own.at[at], self.full.at[self.links.t, at], self.base + 1 + c, self.over
        )

    def pass_copy(self, c):
        part = self.full.at[self.far, self.at(c)]
        return self.links.copy(part, part, self.base + 1 + CHUNKS + c, self.sibling)

    def start_beside(self):
        self.beside_copy().start()

    def start_over(self):
        for c in range(CHUNKS):
            self.over_copy(c).start()

    def came_beside(self):
        self.links.arrived(self.full.at[self.links.t ^ 1], self.base, self.sibling)

    def came_over(self):
        for c in range(CHUNKS):
            self.links.arrived(
                self.full.at[self.far, self.at(c)], self.base + 1 + c, self.over
            )
            self.pass_copy(c).start()

    def came_last(self):
        for c in range(CHUNKS):
            self.links.arrived(
                self.full.at[self.last, self.at(c)], self.base + 1 + CHUNKS + c, self.sibling
            )

    def sent(self):
        self.beside_copy().wait_send()
        for c in range(CHUNKS):
            self.over_copy(c).wait_send()
            self.pass_copy(c).wait_send()


class RowScatter:
    FLOWS = 2 + 4

    def __init__(self, links, base, part, near, near_far, mid, far):
        self.links, self.base, self.part = links, base, part
        self.near, self.near_far, self.mid, self.far = near, near_far, mid, far
        self.sibling, self.over = links.tp_peer(1), links.tp_peer(2)

    def at(self, c):
        rows = self.near.shape[0] // CHUNKS
        return pl.ds(c * rows, rows)

    def first_copy(self):
        return self.links.copy(
            self.part.at[self.links.t ^ 3], self.near_far, self.base, self.sibling
        )

    def second_copy(self):
        return self.links.copy(
            self.part.at[self.links.t ^ 1], self.near, self.base + 1, self.sibling
        )

    def over_copy(self, c):
        at = self.at(c)
        return self.links.copy(
            self.mid.at[at], self.far.at[at], self.base + 2 + c, self.over
        )

    def send_over(self):
        self.links.arrived(self.near_far, self.base, self.sibling)
        for c in range(CHUNKS):
            at = self.at(c)
            self.mid[at] = (
                self.part[self.links.t ^ 2, at].astype(f32) + self.near_far[at].astype(f32)
            ).astype(bf16)
            self.over_copy(c).start()

    def came_beside(self):
        self.links.arrived(self.near, self.base + 1, self.sibling)

    def came_over(self, c):
        at = self.at(c)
        self.links.arrived(self.far.at[at], self.base + 2 + c, self.over)
        return (
            self.part[self.links.t, at].astype(f32)
            + self.near[at].astype(f32)
            + self.far[at].astype(f32)
        )

    def sent(self):
        self.first_copy().wait_send()
        self.second_copy().wait_send()
        for c in range(CHUNKS):
            self.over_copy(c).wait_send()


def cut(refs, *counts):
    out, at = [], 0
    for count in counts:
        out.append(refs[at : at + count])
        at += count
    return out


def self_forward_kernel(prefix_len, count, *refs):
    ins, own, outs, full, stage, scratch = cut(refs, 10, count, 8, count, count + 1, 13)
    x, memory, pre_cross, wq, wk, wv, wo, pre, seg_col, seg_row = ins
    q_out, k_out, v_out, a_out, l_out, resid, m_full, pre_full = outs
    x_full, part, kept, bias, near, near_far, mid, far, send, recv, local, m_local, pre_local = scratch
    links = Links(send, recv)
    t = links.t
    block, lanes = x.shape[0], q_out.shape[1]
    weights = WeightGather(links, 0, 1, own, full, stage[:count], local)
    at = count * FLOWS
    x_rows = RowGather(links, at, x, x_full)
    m_rows = RowGather(links, at + RowGather.FLOWS, memory, m_full)
    at += 2 * RowGather.FLOWS
    sums = RowScatter(links, at, part, near, near_far, mid, far)
    at += RowScatter.FLOWS
    m_in = pltpu.make_async_copy(memory, stage[count], m_local.at[0])
    m_keep = pltpu.make_async_copy(stage[count], m_full.at[t], m_local.at[1])
    pre_keep = pltpu.make_async_copy(pre_cross, pre_full.at[t], pre_local.at[0])
    pre_sends = [
        links.copy(pre_cross, pre_full.at[t], at + m - 1, links.tp_peer(m)) for m in (1, 2, 3)
    ]

    kept[...] = jnp.zeros_like(kept)
    greet(
        [links.tp_peer(m) for m in (1, 2, 3)]
        + [links.line_peer(d) for d in range(1, LINE)]
        + [links.side_peer()]
    )
    x_rows.start_over()
    x_rows.start_beside()
    m_rows.start_beside()
    m_in.start()
    pre_keep.start()
    for one in pre_sends:
        one.start()
    for i in range(count):
        weights.start_beside(i)

    for target, at in ((k_out, 0), (v_out, PRE_PACK)):
        target[0:PRE_PACK] = pre[at : at + PRE_PACK]
        target[PRE_PACK:PRE] = jnp.zeros((PRE - PRE_PACK, lanes), bf16)

    def project(rows, index):
        at = pl.multiple_of(index * block, block)
        q_out[pl.ds(at, block)] = (SCALE * nn(rows, wq[...])).astype(bf16)
        k_out[pl.ds(PRE + at, block)] = nn(rows, wk[...]).astype(bf16)
        v_out[pl.ds(PRE + at, block)] = nn(rows, wv[...]).astype(bf16)

    project(x[...], t)
    x_rows.came_beside()
    project(x_full[t ^ 1], t ^ 1)
    m_in.wait()
    m_keep.start()
    for i in range(count):
        weights.keep_own(i)
    x_rows.came_over()
    for i in range(count):
        weights.start_over(i)
    m_rows.start_over()
    project(x_full[t ^ 2], t ^ 2)
    x_rows.came_last()
    project(x_full[t ^ 3], t ^ 3)

    @pl.loop(0, 4)
    def _(order):
        here = t ^ (3 - order)
        for i in range(4):
            keys = PRE + (i + 1) * block
            shape = (block, keys)

            @pl.when(here == i)
            def _():
                bias[:, 0:keys] = mask_bias(
                    seg_col[i * block : (i + 1) * block],
                    seg_row[:, 0:keys],
                    i * block + lax.broadcasted_iota(jnp.int32, shape, 0),
                    lax.broadcasted_iota(jnp.int32, shape, 1),
                    prefix_len,
                )

                @pl.loop(0, lanes // PAIR)
                def _(j):
                    cols = pl.ds(pl.multiple_of(j * PAIR, PAIR), PAIR)
                    mixture, logs = pair_forward(
                        q_out[i * block : (i + 1) * block, cols],
                        k_out[0:keys, cols],
                        v_out[0:keys, cols],
                        bias[:, 0:keys],
                    )
                    a_out[i, :, cols] = mixture
                    keep_logs(kept, logs, j)

        l_out[here] = kept[...].T[0:8]
        part[here] = nn(a_out[here], wo[...]).astype(bf16)

        @pl.when(order == 0)
        def _():
            sums.first_copy().start()
            for i in range(count):
                weights.came_over(i)

        @pl.when(order == 1)
        def _():
            sums.send_over()

        @pl.when(order == 2)
        def _():
            sums.second_copy().start()
            for i in range(count):
                weights.along(i, 0)

    for i in range(count):
        weights.along(i, 1)
    m_rows.came_over()
    for i in range(count):
        weights.along(i, 2)
    sums.came_beside()
    for i in range(count - 1):
        weights.complete(i)
    for c in range(CHUNKS):
        rows = sums.at(c)
        resid[rows] = x[rows].astype(f32) + sums.came_over(c)
    weights.complete(count - 1)
    m_rows.came_beside()
    m_rows.came_last()
    for m, one in zip((1, 2, 3), pre_sends):
        links.copy(
            pre_full.at[t ^ m], pre_full.at[t ^ m], small_base(count) + m - 1, links.tp_peer(m)
        ).wait_recv()
        one.wait_send()
    for i in range(count):
        weights.finish(i)
    x_rows.sent()
    m_rows.sent()
    sums.sent()
    m_keep.wait()
    pre_keep.wait()


def small_base(count):
    return count * FLOWS + 2 * RowGather.FLOWS + RowScatter.FLOWS


def self_forward(prefix_len, x, memory, pre_cross, own_weights, pre, seg_col, seg_row, weights):
    n = 4
    count = len(weights)
    block, width = x.shape
    lanes = own_weights[0].shape[1]
    seq = n * block
    out = jax.ShapeDtypeStruct
    flows = small_base(count) + 3
    outs = (
        out((seq, lanes), bf16),
        out((PRE + seq, lanes), bf16),
        out((PRE + seq, lanes), bf16),
        out((n, block, lanes), bf16),
        out((n, 8, block), f32),
        out((block, width), f32),
        out((n, block, width), bf16),
        out((n,) + pre_cross.shape, bf16),
    ) + tuple(out((n,) + a.shape, a.dtype) for a in weights)
    a = pl.BlockSpec(memory_space=pltpu.HBM)
    rows = VMEM((block, width), bf16)
    given = (x, memory, pre_cross, *own_weights, pre, seg_col, seg_row)
    in_specs = [whole_spec(g.shape) for g in given]
    in_specs[1] = a
    return pl.pallas_call(
        functools.partial(self_forward_kernel, prefix_len, count),
        grid=(1,),
        out_shape=outs,
        in_specs=in_specs + [a] * count,
        out_specs=[whole_spec(o.shape) for o in outs[:6]] + [a] * (2 + count),
        scratch_shapes=[VMEM(w.shape, w.dtype) for w in weights]
        + [rows]
        + [
            VMEM((n, block, width), bf16),
            VMEM((n, block, width), bf16),
            VMEM((block, 128), f32),
            VMEM((block, PRE + seq), f32),
            rows,
            rows,
            rows,
            rows,
            pltpu.SemaphoreType.DMA((flows,)),
            pltpu.SemaphoreType.DMA((flows,)),
            pltpu.SemaphoreType.DMA((2 * count,)),
            pltpu.SemaphoreType.DMA((2,)),
            pltpu.SemaphoreType.DMA((1,)),
        ],
        compiler_params=pltpu.CompilerParams(
            collective_id=0, has_side_effects=True, vmem_limit_bytes=48 << 20
        ),
        name="self_forward",
    )(*given, *weights)


def doublings(count):
    levels = 0
    while (1 << levels) < count:
        levels += 1
    return levels


def cross_backward_kernel(
    prefix_len, levels, dr2, v1, q, k, v, a, logs, wq, wk, wv, wo, seg_row, seg_col, gain, vecs_in, g,
    dr1, dr1_full, dm, pre_grad, vecs, piece,
    dr1_low, dr2_low, bias, da, dq, dk, dv, total, s1, h, xb, h2, zb, p3, yb, hb, send, recv, local,
):
    step = pl.program_id(0)
    steps = pl.num_programs(0)
    block, lanes = q.shape[1:]
    keys = k.shape[1]
    links = Links(send, recv)
    t = links.t
    rows = RowGather(links, 0, dr1_low, dr1_full)
    keep = pltpu.make_async_copy(dr1_low, dr1_full.at[t], local.at[0])
    reduce = AdapterReduce(links, RowGather.FLOWS, levels, g, s1, h, xb, h2, zb, p3, yb, hb)

    @pl.when(step == 0)
    def _():
        greet(
            [links.tp_peer(1), links.tp_peer(2)]
            + [links.line_peer(d) for d in range(1, LINE)]
            + [links.side_peer()]
            + reduce.groups
        )
        reduce.phase(0)
        dr2_low[...] = dr2[...].astype(bf16)
        total[...] = jnp.zeros_like(total)
        bias[...] = mask_bias(
            seg_row[...],
            seg_col[...],
            None,
            lax.broadcasted_iota(jnp.int32, (keys, block), 0),
            prefix_len,
        )

    da[...] = nt(dr2_low[...], wo[0]).astype(bf16)

    @pl.loop(0, lanes // PAIR)
    def _(j):
        cols = pl.ds(pl.multiple_of(j * PAIR, PAIR), PAIR)
        dq_pair, dk_pair, dv_pair = pair_backward(
            q[0, :, cols],
            k[0, :, cols],
            v[0, :, cols],
            a[0, :, cols],
            da[:, cols],
            [logs[0, pl.ds(2 * j + i, 1)] for i in range(2)],
            bias[...],
        )
        dq[:, cols] = dq_pair
        pre_grad[0, 0:PRE_PACK, cols] = dk_pair[0:PRE_PACK]
        pre_grad[0, PRE_PACK : 2 * PRE_PACK, cols] = dv_pair[0:PRE_PACK]
        dk[step, :, cols] = dk_pair[PRE:].astype(bf16)
        dv[step, :, cols] = dv_pair[PRE:].astype(bf16)

    total[...] += nt(dq[...], wq[0])
    for number in range(3):

        @pl.when(step == number)
        def _():
            reduce.phase(number + 1)

    @pl.when(step == steps - 1)
    def _():
        n, spread = norm_parts(v1[...])
        grad, gain_part, shift_part = norm_back(
            dr2[...] + SCALE * total[...], gain[0:1], n, spread
        )
        dr1[...] = grad
        dr1_low[...] = grad.astype(bf16)
        rows.start_over()
        rows.start_beside()
        keep.start()
        vecs[...] = vecs_in[...]
        vecs[0:1] = gain_part
        vecs[3:4] = shift_part
        piece[...] = reduce.result()

        @pl.loop(0, 4)
        def _(i):
            at = pl.ds(pl.multiple_of(i * block, block), block)
            value = None
            for shard in range(dk.shape[0]):
                term = nt(dk[shard, at], wk[shard]) + nt(dv[shard, at], wv[shard])
                value = term if value is None else value + term
            dm[i] = value.astype(bf16)

        rows.came_over()
        rows.came_beside()
        rows.came_last()
        rows.sent()
        keep.wait()


def cross_backward(
    prefix_len, row_count, dr2, v1, q, k, v, a, logs, weights, seg_row, seg_col, gain, vecs, grads
):
    wq, wk, wv, wo = weights
    n, block, lanes = q.shape
    keys = k.shape[1]
    width = dr2.shape[1]
    levels = doublings(row_count // GROUP)
    part = grads.shape[1] // GROUP
    half = (2, LINE, part, width)
    g = grads.reshape((2,) + half)
    out = jax.ShapeDtypeStruct
    outs = (
        out((block, width), f32),
        out((n, block, width), bf16),
        out((n, block, width), bf16),
        out((n, 2 * PRE_PACK, lanes), f32),
        out((8, width), f32),
        out((part, width), bf16),
    )
    out_specs = [whole_spec(o.shape) for o in outs]
    out_specs[1] = pl.BlockSpec(memory_space=pltpu.HBM)
    out_specs[3] = shard_spec(outs[3].shape)
    flows = RowGather.FLOWS + 2 + LINE + levels
    return pl.pallas_call(
        functools.partial(cross_backward_kernel, prefix_len, levels),
        grid=(n,),
        out_shape=outs,
        in_specs=[whole_spec(dr2.shape), whole_spec(v1.shape)]
        + [shard_spec(x.shape) for x in (q, k, v, a, logs, wq)]
        + [whole_spec(wk.shape), whole_spec(wv.shape), shard_spec(wo.shape)]
        + [whole_spec(x.shape) for x in (seg_row, seg_col, gain, vecs, g)],
        out_specs=out_specs,
        scratch_shapes=[
            VMEM((block, width), bf16),
            VMEM((block, width), bf16),
            VMEM((keys, block), f32),
            VMEM((block, lanes), bf16),
            VMEM((block, lanes), bf16),
            VMEM((n, keys - PRE, lanes), bf16),
            VMEM((n, keys - PRE, lanes), bf16),
            VMEM((block, width), f32),
            VMEM(half, bf16),
            VMEM(half, bf16),
            VMEM(half[1:], bf16),
            VMEM(half[1:], bf16),
            VMEM((LINE - 1, part, width), bf16),
            VMEM((part, width), bf16),
            VMEM((part, width), bf16),
            VMEM((max(1, 2 * levels), part, width), bf16),
            pltpu.SemaphoreType.DMA((flows,)),
            pltpu.SemaphoreType.DMA((flows,)),
            pltpu.SemaphoreType.DMA((1,)),
        ],
        compiler_params=pltpu.CompilerParams(
            collective_id=2, has_side_effects=True, vmem_limit_bytes=58 << 20
        ),
        name="cross_backward",
    )(dr2, v1, q, k, v, a, logs, wq, wk, wv, wo, seg_row, seg_col, gain, vecs, g)


class Doubling:
    def __init__(self, links, base, levels, outgo, income):
        self.links, self.base, self.levels = links, base, levels
        self.outgo, self.income = outgo, income

    def move(self, level):
        return self.links.copy(
            self.outgo.at[level],
            self.income.at[level],
            self.base + level,
            (self.links.row ^ (1 << level), self.links.t),
        )

    def begin(self, value):
        self.outgo[0] = value
        self.move(0).start()

    def value(self, level):
        self.move(level).wait()
        return self.outgo[level] + self.income[level]

    def step(self, level):
        value = self.value(level)
        self.outgo[level + 1] = value
        self.move(level + 1).start()


def self_backward_kernel(
    prefix_len, levels, dr1_full, dr1, q, k, v, a, logs, wq, wk, wv, wo, seg_row, seg_col,
    dm, piece, cross, vecs,
    tokens_grad, memory_grad, adapter, self_pre, sums,
    part, bias, da, dq, dk, dv, near, near_far, mid, far, m_near, m_near_far, m_mid, m_far,
    cross_in, vecs_in, outgo, income, pre_outgo, pre_income, send, recv,
):
    seq, lanes = q.shape
    block = seq // 4
    links = Links(send, recv)
    t = links.t
    at = 0
    spread = AdapterSpread(links, at, adapter)
    at += FLOWS
    m_sums = RowScatter(links, at, dm, m_near, m_near_far, m_mid, m_far)
    at += RowScatter.FLOWS
    x_sums = RowScatter(links, at, part, near, near_far, mid, far)
    at += RowScatter.FLOWS
    total = Doubling(links, at, levels, outgo, income)
    at += levels
    pre_total = Doubling(links, at, levels, pre_outgo, pre_income)
    at += levels

    def exchange(m):
        peer = links.tp_peer(m)
        return (
            links.copy(cross.at[t ^ m], cross_in.at[t], at + 2 * (m - 1), peer),
            links.copy(vecs, vecs_in.at[t], at + 2 * (m - 1) + 1, peer),
        )

    greet(
        [links.tp_peer(m) for m in (1, 2, 3)]
        + [links.line_peer(d) for d in range(1, LINE)]
        + [links.side_peer()]
        + [(links.row ^ (1 << level), t) for level in range(doublings(GROUP), levels)]
    )
    m_sums.first_copy().start()
    m_sums.second_copy().start()
    for m in (1, 2, 3):
        for one in exchange(m):
            one.start()
    adapter[spread.half, links.b, links.a] = piece[...]
    spread.spread(0)
    cross_in[t] = cross[t]
    vecs_in[t] = vecs[...]
    dk[...] = jnp.zeros_like(dk)
    dv[...] = jnp.zeros_like(dv)

    for i in reversed(range(4)):
        rows = slice(i * block, (i + 1) * block)
        keys = PRE + (i + 1) * block
        shape = (keys, block)
        bias[0:keys] = mask_bias(
            seg_row[:, rows],
            seg_col[0:keys],
            i * block + lax.broadcasted_iota(jnp.int32, shape, 1),
            lax.broadcasted_iota(jnp.int32, shape, 0),
            prefix_len,
        )
        da[...] = nt(dr1_full[i], wo[...]).astype(bf16)

        @pl.loop(0, lanes // PAIR)
        def _(j):
            cols = pl.ds(pl.multiple_of(j * PAIR, PAIR), PAIR)
            dq_pair, dk_pair, dv_pair = pair_backward(
                q[rows, cols],
                k[0:keys, cols],
                v[0:keys, cols],
                a[i, :, cols],
                da[:, cols],
                [logs[i, pl.ds(2 * j + o, 1)] for o in range(2)],
                bias[0:keys],
            )
            dq[:, cols] = dq_pair
            dk[0:keys, cols] += dk_pair
            dv[0:keys, cols] += dv_pair

        done = slice(PRE + i * block, PRE + (i + 1) * block)
        part[i] = (
            SCALE * nt(dq[...], wq[...])
            + nt(dk[done].astype(bf16), wk[...])
            + nt(dv[done].astype(bf16), wv[...])
        ).astype(bf16)
        if i == 3:
            m_sums.send_over()
            for m in (1, 2, 3):
                peer = links.tp_peer(m)
                links.arrived(cross_in.at[t ^ m], at + 2 * (m - 1), peer)
                links.arrived(vecs_in.at[t ^ m], at + 2 * (m - 1) + 1, peer)
            value = vecs_in[0] + vecs_in[1] + vecs_in[2] + vecs_in[3]
            pieces = [cross_in[0] + cross_in[1] + cross_in[2] + cross_in[3]] + [
                value[:, o * lanes : (o + 1) * lanes] for o in range(vecs.shape[1] // lanes)
            ]
            total.begin(jnp.concatenate(pieces, axis=0))
        else:
            spread.along(0, 2 - i)
            if i > 0:
                total.step(2 - i)

    x_sums.first_copy().start()
    x_sums.second_copy().start()
    pre_total.begin(jnp.concatenate([dk[0:PRE_PACK], dv[0:PRE_PACK]], axis=0))
    spread.complete(0)
    x_sums.send_over()
    for level in range(2, levels - 1):
        total.step(level)
    sums[...] = total.value(levels - 1)
    for level in range(levels - 1):
        pre_total.step(level)
    m_sums.came_beside()
    for c in range(CHUNKS):
        memory_grad[m_sums.at(c)] = m_sums.came_over(c).astype(bf16)
    x_sums.came_beside()
    for c in range(CHUNKS):
        rows = x_sums.at(c)
        tokens_grad[rows] = (dr1[rows] + x_sums.came_over(c)).astype(bf16)
    self_pre[...] = pre_total.value(levels - 1)
    spread.finish(0)
    m_sums.sent()
    x_sums.sent()
    for m in (1, 2, 3):
        for one in exchange(m):
            one.wait_send()


def self_backward(
    prefix_len, row_count, dr1_full, dr1, q, k, v, a, logs, weights, seg_row, seg_col,
    dm, piece, cross, vecs,
):
    n, block, width = dr1_full.shape
    seq, lanes = q.shape
    levels = doublings(row_count)
    packed = 2 * PRE_PACK
    height = packed + vecs.shape[0] * vecs.shape[1] // lanes
    out = jax.ShapeDtypeStruct
    outs = (
        out((block, width), bf16),
        out((block, width), bf16),
        out((2, 2, LINE) + piece.shape, bf16),
        out((packed, lanes), f32),
        out((height, lanes), f32),
    )
    given = (
        (dr1_full, dr1, q, k, v, a, logs) + tuple(weights) + (seg_row, seg_col, dm, piece, cross, vecs)
    )
    rows = VMEM((block, width), bf16)
    flows = FLOWS + 2 * RowScatter.FLOWS + 2 * levels + 6
    return pl.pallas_call(
        functools.partial(self_backward_kernel, prefix_len, levels),
        grid=(1,),
        out_shape=outs,
        in_specs=[whole_spec(x.shape) for x in given],
        out_specs=[whole_spec(x.shape) for x in outs[:2]]
        + [pl.BlockSpec(memory_space=VMEM)]
        + [whole_spec(x.shape) for x in outs[3:]],
        scratch_shapes=[
            VMEM((n, block, width), bf16),
            VMEM((PRE + seq, block), f32),
            VMEM((block, lanes), bf16),
            VMEM((block, lanes), bf16),
            VMEM((PRE + seq, lanes), f32),
            VMEM((PRE + seq, lanes), f32),
        ]
        + [rows] * 8
        + [
            VMEM((n, packed, lanes), f32),
            VMEM((n,) + vecs.shape, f32),
            VMEM((levels, height, lanes), f32),
            VMEM((levels, height, lanes), f32),
            VMEM((levels, packed, lanes), f32),
            VMEM((levels, packed, lanes), f32),
            pltpu.SemaphoreType.DMA((flows,)),
            pltpu.SemaphoreType.DMA((flows,)),
        ],
        compiler_params=pltpu.CompilerParams(
            collective_id=3, has_side_effects=True, vmem_limit_bytes=58 << 20
        ),
        name="self_backward",
    )(*given)


def per_device(
    row_count,
    tokens, memory, out_grad, dec_segments, src_segments,
    self_query, self_key, self_value, self_out,
    cross_query, cross_key, cross_value, cross_out,
    ffn_in, ffn_out, adapt_down, adapt_down_bias, adapt_up, adapt_up_bias,
    self_prefix, cross_prefix, norm_gain, norm_shift,
):
    seq_local, _, width = tokens.shape
    prefix_len = self_prefix.shape[1]
    lanes = self_query.shape[1]
    adapt = adapt_down.shape[1]
    t = lax.axis_index("tp")
    x, mem, grad_in = (a.reshape(seq_local, width) for a in (tokens, memory, out_grad))

    def pack_prefix(prefix):
        return jnp.pad(prefix, ((0, 0), (0, PRE_PACK - prefix_len), (0, 0))).reshape(
            2 * PRE_PACK, lanes
        )

    def unpack_prefix(packed):
        return packed.reshape(2, PRE_PACK, lanes)[:, :prefix_len]

    seq = dec_segments.shape[1]
    never = jnp.full((1, PRE), -1, jnp.int32)
    dec_row = jnp.concatenate([never, dec_segments], axis=1)
    src_row = jnp.concatenate([never, src_segments], axis=1)
    dec_q = dec_segments
    own_q = lax.dynamic_slice(dec_segments, (0, t * seq_local), (1, seq_local))

    q1, k1, v1_heads, a1, logs1, resid_one, m_full, pre_full, *gathered = self_forward(
        prefix_len, x, mem, pack_prefix(cross_prefix),
        (self_query, self_key, self_value, self_out),
        pack_prefix(self_prefix), dec_q.reshape(seq, 1), dec_row,
        (cross_query, cross_key, cross_value, cross_out, ffn_in),
    )
    cross_weights = gathered[:4]
    w_in = gathered[4]
    m_full = m_full.reshape(seq, width)
    q2, k2, v2_heads, a2, logs2, resid_two, w_out = cross_forward(
        prefix_len, resid_one, m_full, cross_weights, pre_full,
        own_q.reshape(seq_local, 1), src_row, norm_gain, norm_shift, ffn_out,
    )
    output, dr2, grads, vecs = feed_forward(
        resid_two, grad_in, w_in, w_out,
        adapt_down, adapt_down_bias.reshape(1, adapt), adapt_up, adapt_up_bias.reshape(1, width),
        norm_gain, norm_shift,
    )
    dr1, dr1_full, dm, cross_pre_part, vecs, piece = cross_backward(
        prefix_len, row_count, dr2, resid_one, q2, k2, v2_heads, a2, logs2, cross_weights,
        own_q, src_row.reshape(PRE + seq, 1), norm_gain, vecs, grads,
    )
    tokens_grad, memory_grad, adapter, self_pre, sums = self_backward(
        prefix_len, row_count, dr1_full, dr1, q1, k1, v1_heads, a1, logs1,
        (self_query, self_key, self_value, self_out), dec_q, dec_row.reshape(PRE + seq, 1),
        dm, piece, cross_pre_part, vecs,
    )
    adapter = adapter.reshape(2 * adapt, width)
    cross_pre = sums[: 2 * PRE_PACK]
    vecs = jnp.moveaxis(sums[2 * PRE_PACK :].reshape(-1, 8, lanes), 0, 1).reshape(8, width)
    local = tokens.shape
    return (
        output.reshape(local),
        tokens_grad.reshape(local),
        memory_grad.reshape(local),
        unpack_prefix(self_pre),
        unpack_prefix(cross_pre),
        vecs[0:3],
        vecs[3:6],
        adapter[adapt:].T.astype(f32),
        vecs[7, :adapt],
        adapter[:adapt].astype(f32),
        vecs[6],
    )


def solution(mesh):
    placed = (
        (P("tp", "rows", None),) * 3
        + (P("rows", None),) * 2
        + (P(None, "tp"),) * 3
        + (P("tp", None),)
        + (P(None, "tp"),) * 3
        + (P("tp", None),)
        + (P(None, "tp"), P("tp", None))
        + (P(),) * 4
        + (P(None, None, "tp"),) * 2
        + (P(),) * 2
    )
    return jax.shard_map(
        functools.partial(per_device, mesh.shape["rows"]),
        mesh=mesh,
        in_specs=placed,
        out_specs=(P("tp", "rows", None),) * 3 + (P(None, None, "tp"),) * 2 + (P(),) * 6,
        check_vma=False,
    )
```

profile of v0, /device:TPU:0, one launch (start us, length us, event | category | flops | bytes accessed | tf_op | source)
XLA Modules:
  0.0 282.2 jit_solution(13944800942888138601)
XLA Ops:
  0.6 0.7 pad_bitcast_fusion
  1.4 0.9 copy.43.refs_8_
  2.3 0.8 copy.54
  3.0 0.8 copy.55
  3.8 0.0 copy-start.2
  3.8 1.0 copy-done.2
  4.9 0.0 copy-start.3
  4.9 1.0 copy-done.3
  5.9 0.0 copy-start.4
  5.9 1.0 copy-done.4
  6.9 0.0 copy-start.5
  7.0 1.0 copy-done.5
  8.0 0.0 copy-start.7
  8.0 1.0 copy-done.7
  9.0 0.0 copy-start.8
  9.0 1.0 copy-done.8
  10.1 0.0 copy-start.9
  10.1 1.0 copy-done.9
  11.1 0.0 copy-start.10
  11.1 1.0 copy-done.10
  12.2 0.0 copy-start.23
  12.2 0.0 copy-start.15
  12.2 0.0 copy-start.16
  12.2 79.7 %self_forward.1 = (bf16[1024,256]{1,0:T(8,128)(2,1)S(1)}, bf16[1152,256]{1,0:T(8,128)(2,1)}, bf16[1152,256]{1,0:T(8,128)(2,1)}, bf16[4,256,256]{2,1,0:T(8,128)(2...) custom-call(bf16[256,1024]{1,0:T(8,128)(2,1)S(1)} %bitcast.41, ...), custom_call_target="tpu_custom_call" | custom-call | tf_op jit(solution)/shard_map/self_forward/pallas_call | solution.py:911
  91.9 0.0 copy-start.11
  91.9 0.8 copy-done.11
  92.7 0.0 copy-start.12
  92.7 0.8 copy-done.12
  93.5 0.0 copy-start.17
  93.5 0.6 copy-done.17
  94.1 0.0 copy-done.23
  94.1 0.1 copy.44.seg_col
  94.3 0.0 copy-done.15
  94.3 0.0 copy-done.16
  94.3 0.0 copy-start
  94.3 1.2 copy-done
  95.5 1.6 copy-done.1
  97.1 41.3 %cross_forward.1 = (bf16[4,256,256]{2,1,0:T(8,128)(2,1)S(1)}, bf16[4,1152,256]{2,1,0:T(8,128)(2,1)}, bf16[4,1152,256]{2,1,0:T(8,128)(2,1)}, bf16[4,256,256]{2,1,...) custom-call(f32[256,1024]{1,0:T(8,128)S(1)} %copy-done, ...), custom_call_target="tpu_custom_call" | custom-call | tf_op jit(solution)/shard_map/cross_forward/pallas_call | solution.py:215
  138.4 0.0 copy-start.6
  138.4 1.0 copy-done.6
  139.4 0.8 copy-done.13
  140.2 0.8 copy-done.14
  141.0 0.6 copy-done.18
  141.6 23.6 %feed_forward.1 = (bf16[256,1024]{1,0:T(8,128)(2,1)}, f32[256,1024]{1,0:T(8,128)}, bf16[2,512,1024]{2,1,0:T(8,128)(2,1)}, f32[8,1024]{1,0:T(8,128)}) custom-call(f32[256,1024]{1,0:T(8,128)} %copy-done.6, bf16[256,1024]{1,0:T(8,128)(2,1)} %bitcast.47, bf16[4,1024,1024]{2,1,0:T(8,128)(2,1)} %get-tuple-element.54.w_in, ...), custom_call_target="tpu_custom_call" | custom-call | tf_op jit(solution)/shard_map/feed_forward/pallas_call | solution.py:310
  165.2 0.6 constant_dynamic-slice_fusion.seg_row
  165.8 1.1 copy.45.seg_col
  166.8 55.3 %cross_backward.1 = (f32[256,1024]{1,0:T(8,128)}, bf16[4,256,1024]{2,1,0:T(8,128)(2,1)}, bf16[4,256,1024]{2,1,0:T(8,128)(2,1)}, f32[4,64,256]{2,1,0:T(8,128)}, f...) custom-call(f32[256,1024]{1,0:T(8,128)} %get-tuple-element.57.dr2, f32[256,1024]{1,0:T(8,128)} %get-tuple-element.46.v1, ...), custom_call_target="tpu_custom_call" | custom-call | tf_op jit(solution)/shard_map/cross_backward/pallas_call | solution.py:1065
  222.2 1.1 copy.46.seg_col
  223.3 48.6 %self_backward.1 = (bf16[256,1024]{1,0:T(8,128)(2,1)}, bf16[256,1024]{1,0:T(8,128)(2,1)}, bf16[2,2,4,64,1024]{4,3,2,1,0:T(8,128)(2,1)}, f32[64,256]{1,0:T(8,128)}, f32[96,256]{1,0:T(8,128)}) custom-call(bf16[4,256,1024]{2,1,0:T(8,128)(2,1)} %get-tuple-element.65.dr1_full, f32[256,1024]{1,0:T(8,128)} %get-tuple-element.66.dr1, bf16[1024,256]{1,0:T(8,128)(2,1)} %copy-done.11, ...), custom_call_target="tpu_custom_call" | custom-call | tf_op jit(solution)/shard_map/self_backward/pallas_call | solution.py:1276
  271.9 1.8 fusion
  273.7 0.3 bitcast_convert_fusion.1
  274.0 1.8 copy.51
  275.8 1.6 bitcast_convert_fusion
  277.5 0.0 copy-done.21
  277.5 0.7 copy.53
  278.1 0.6 fusion.2
  278.8 0.6 slice.56
  279.4 0.6 slice.55
  279.9 0.0 copy-done.22
  280.0 0.7 copy.52
  280.6 0.0 copy-done.20
  280.6 0.8 copy.58
  281.4 0.0 copy-done.19
  281.4 0.8 copy.59
  (13 shorter events, 0.0 us)
Async XLA Ops:
  3.8 1.0 copy-start.2
  4.9 1.0 copy-start.3
  5.9 1.0 copy-start.4
  6.9 1.0 copy-start.5
  8.0 1.0 copy-start.7
  9.0 1.0 copy-start.8
  10.1 1.0 copy-start.9
  11.1 1.0 copy-start.10
  12.2 82.0 %copy-start.23 = (s32[1,1024]{1,0:T(1,128)S(1)}, s32[1,1024]{1,0:T(1,128)}, u32[]{:S(2)}) copy-start(s32[1,1024]{1,0:T(1,128)} %seg_row.1) | copy-start | bytes 12292
  12.2 82.1 %copy-start.15 = (f32[3,1024]{1,0:T(4,128)S(1)}, f32[3,1024]{1,0:T(4,128)}, u32[]{:S(2)}) copy-start(f32[3,1024]{1,0:T(4,128)} %gain.5) | copy-start | bytes 36868
  12.2 82.1 %copy-start.16 = (f32[3,1024]{1,0:T(4,128)S(1)}, f32[3,1024]{1,0:T(4,128)}, u32[]{:S(2)}) copy-start(f32[3,1024]{1,0:T(4,128)} %shift.3) | copy-start | bytes 36868
  91.9 0.8 copy-start.11
  92.7 0.8 copy-start.12
  93.5 0.6 copy-start.17
  94.3 1.2 copy-start
  95.5 1.6 copy-start.1
  138.4 1.0 copy-start.6
  139.4 0.8 copy-start.13
  140.2 0.8 copy-start.14
  141.0 0.6 copy-start.18
  275.8 1.6 copy-start.21
  275.8 4.1 %copy-start.22 = (f32[64,256]{1,0:T(8,128)S(1)}, f32[64,256]{1,0:T(8,128)}, u32[]{:S(2)}) copy-start(f32[64,256]{1,0:T(8,128)} %get-tuple-element.78) | copy-start | bytes 196612
  275.8 4.8 %copy-start.20 = (bf16[256,1024]{1,0:T(8,128)(2,1)S(1)}, bf16[256,1024]{1,0:T(8,128)(2,1)}, u32[]{:S(2)}) copy-start(bf16[256,1024]{1,0:T(8,128)(2,1)} %get-tuple-element.76) | copy-start | bytes 1572868
  275.8 5.6 %copy-start.19 = (bf16[256,1024]{1,0:T(8,128)(2,1)S(1)}, bf16[256,1024]{1,0:T(8,128)(2,1)}, u32[]{:S(2)}) copy-start(bf16[256,1024]{1,0:T(8,128)(2,1)} %get-tuple-element.77) | copy-start | bytes 1572868
where the time goes:
time: 283 us; the launch traced here: 282 us
  Pallas kernels  249 us (88%)
  local copies, waits for them, and re-layouts  30.9 us (11%)
    pallas_call x1, Pallas kernels, self_forward(): pl.pallas_call(functools.partial(self_forward_kernel, prefix_len, count),...  79.7 us
    pallas_call x1, Pallas kernels, cross_backward(): pl.pallas_call(functools.partial(cross_backward_kernel, prefix_len, level...  55.3 us
    pallas_call x1, Pallas kernels, self_backward(): pl.pallas_call(functools.partial(self_backward_kernel, prefix_len, levels...  48.6 us
    pallas_call x1, Pallas kernels, cross_forward(): pl.pallas_call(functools.partial(cross_forward_kernel, prefix_len), grid=...  41.3 us
    pallas_call x1, Pallas kernels, feed_forward(): pl.pallas_call(feed_forward_kernel, grid=(2 * n,), out_shape=outs, in_spe...  23.6 us
    unnamed x54, local copies, waits for them, and re-layouts  21 us

commit v1 on v0

--- a/solution.py
+++ b/solution.py
@@ -15,6 +15,7 @@
 LINE = 4
 MASKED = -1000000000.0
 EPSILON = 1e-05
+VMEM_BYTES = 62 << 20
 SCALE = HEAD**-0.5
 f32 = jnp.float32
 bf16 = jnp.bfloat16
@@ -59,11 +60,19 @@
     return (lax.broadcasted_iota(jnp.int32, shape, 1) // HEAD) == h
 
 
-def mask_bias(seg_q, seg_k, q_index, k_index, prefix_len):
+def column(row):
+    return jnp.broadcast_to(row, (8, row.shape[1])).T[:, 0:1]
+
+
+def prefix_bias(shape, axis, prefix_len):
+    return jnp.where(lax.broadcasted_iota(jnp.int32, shape, axis) < prefix_len, 0.0, MASKED)
+
+
+def mask_bias(seg_q, seg_k, shape, key_axis, first_query):
     keep = seg_q == seg_k
-    if q_index is not None:
-        keep = keep & (k_index - PRE <= q_index)
-    keep = keep | (k_index < prefix_len)
+    if first_query is not None:
+        query = first_query + lax.broadcasted_iota(jnp.int32, shape, 1 - key_axis)
+        keep = keep & (lax.broadcasted_iota(jnp.int32, shape, key_axis) <= query)
     return jnp.where(keep, 0.0, MASKED)
 
 
@@ -113,14 +122,14 @@
 
 
 def cross_forward_kernel(
-    prefix_len, v1, memory, wq, wk, wv, wo, pre, seg_col, seg_row, gain, shift, own,
+    prefix_len, v1, memory, wq, wk, wv, wo, pre, dec, src, gain, shift, own,
     q_out, k_out, v_out, a_out, l_out, v2, full, n1_low, bias, kept, stage, send, recv, local,
 ):
     step = pl.program_id(0)
     block, lanes = q_out.shape[1:]
     keys = k_out.shape[1]
     links = Links(send, recv)
-    weights = WeightGather(links, 0, 2, [own], [full], [stage], local)
+    weights = WeightGather(links, 0, [2, 2], *chunked([own], [full], [stage]), local)
 
     @pl.when(step == 0)
     def _():
@@ -129,8 +138,10 @@
             + [links.line_peer(d) for d in range(1, LINE)]
             + [links.side_peer()]
         )
-        weights.start_over(0)
-        weights.start_beside(0)
+        for i in range(2):
+            weights.start_over(i)
+        for i in range(2):
+            weights.start_beside(i)
 
     @pl.when(step == 0)
     def _():
@@ -139,12 +150,10 @@
         v2[...] = normed
         n1_low[...] = normed.astype(bf16)
         kept[...] = jnp.zeros_like(kept)
-        bias[...] = mask_bias(
-            seg_col[...],
-            seg_row[...],
-            None,
-            lax.broadcasted_iota(jnp.int32, (block, keys), 1),
-            prefix_len,
+        own_queries = dec[:, pl.ds(pl.multiple_of(links.t * block, block), block)]
+        bias[:, 0:PRE] = prefix_bias((block, PRE), 1, prefix_len)
+        bias[:, PRE:] = mask_bias(
+            column(own_queries), src[...], (block, keys - PRE), 1, None
         )
 
     q_out[0] = (SCALE * nn(n1_low[...], wq[0])).astype(bf16)
@@ -159,36 +168,38 @@
         k_out[0, pl.ds(PRE + at, block)] = nn(rows, wk[0]).astype(bf16)
         v_out[0, pl.ds(PRE + at, block)] = nn(rows, wv[0]).astype(bf16)
 
-    @pl.loop(0, lanes // PAIR)
-    def _(j):
-        cols = pl.ds(pl.multiple_of(j * PAIR, PAIR), PAIR)
+    events = {
+        0: [lambda: weights.keep_own(0), lambda: weights.keep_own(1), lambda: weights.came_over(0)],
+        2: [lambda: weights.came_over(1)],
+        3: [lambda: weights.along(0, 0)],
+        4: [lambda: weights.along(1, 0), lambda: weights.along(0, 1)],
+        5: [lambda: weights.along(1, 1)],
+        6: [lambda: weights.along(0, 2)],
+        7: [lambda: weights.along(1, 2)],
+    }
+    for j in range(lanes // PAIR):
+        cols = slice(j * PAIR, (j + 1) * PAIR)
         mixture, logs = pair_forward(
             q_out[0, :, cols], k_out[0, :, cols], v_out[0, :, cols], bias[...]
         )
         a_out[0, :, cols] = mixture
         keep_logs(kept, logs, j)
+        for shard in range(4):
+
+            @pl.when(step == shard)
+            def _():
+                for event in events.get(2 * shard + j, []):
+                    event()
 
     l_out[0] = kept[...].T[0:8]
     v2[...] += nn(a_out[0], wo[0])
 
-    @pl.when(step == 0)
-    def _():
-        weights.keep_own(0)
-        weights.came_over(0)
-
-    @pl.when(step == 1)
-    def _():
-        weights.along(0, 0)
-
-    @pl.when(step == 2)
-    def _():
-        weights.along(0, 1)
-
     @pl.when(step == pl.num_programs(0) - 1)
     def _():
-        weights.along(0, 2)
-        weights.complete(0)
-        weights.finish(0)
+        for i in range(2):
+            weights.complete(i)
+        for i in range(2):
+            weights.finish(i)
 
 
 def whole_spec(shape):
@@ -199,7 +210,7 @@
     return pl.BlockSpec((1,) + shape[1:], lambda i: (index(i), 0, 0))
 
 
-def cross_forward(prefix_len, v1, memory, weights, pre, seg_col, seg_row, gain, shift, own):
+def cross_forward(prefix_len, v1, memory, weights, pre, dec, src, gain, shift, own):
     wq, wk, wv, wo = weights
     n, width, lanes = wq.shape
     block = v1.shape[0]
@@ -218,7 +229,7 @@
         out_shape=outs + (out((block, width), f32), out((n,) + own.shape, own.dtype)),
         in_specs=[whole_spec(v1.shape), whole_spec(memory.shape)]
         + [shard_spec(a.shape) for a in (wq, wk, wv, wo, pre)]
-        + [whole_spec(a.shape) for a in (seg_col, seg_row, gain, shift)]
+        + [whole_spec(a.shape) for a in (dec, src, gain, shift)]
         + [pl.BlockSpec(memory_space=pltpu.HBM)],
         out_specs=[shard_spec(a.shape) for a in outs]
         + [whole_spec((block, width)), pl.BlockSpec(memory_space=pltpu.HBM)],
@@ -227,15 +238,15 @@
             VMEM((block, PRE + seq), f32),
             VMEM((block, 128), f32),
             VMEM(own.shape, own.dtype),
-            pltpu.SemaphoreType.DMA((FLOWS,)),
-            pltpu.SemaphoreType.DMA((FLOWS,)),
-            pltpu.SemaphoreType.DMA((2,)),
+            pltpu.SemaphoreType.DMA((2 * FLOWS,)),
+            pltpu.SemaphoreType.DMA((2 * FLOWS,)),
+            pltpu.SemaphoreType.DMA((4,)),
         ],
         compiler_params=pltpu.CompilerParams(
-            collective_id=1, has_side_effects=True, vmem_limit_bytes=48 << 20
+            collective_id=1, has_side_effects=True, vmem_limit_bytes=VMEM_BYTES
         ),
         name="cross_forward",
-    )(v1, memory, wq, wk, wv, wo, pre, seg_col, seg_row, gain, shift, own)
+    )(v1, memory, wq, wk, wv, wo, pre, dec, src, gain, shift, own)
 
 
 def feed_forward_kernel(
@@ -323,7 +334,7 @@
             VMEM((n, block, inner), f32),
             VMEM((block, width), f32),
         ],
-        compiler_params=pltpu.CompilerParams(vmem_limit_bytes=56 << 20),
+        compiler_params=pltpu.CompilerParams(vmem_limit_bytes=VMEM_BYTES),
         name="feed_forward",
     )(v2, out_grad, w_in, w_out, down, down_bias, up, up_bias, gain, shift)
 
@@ -437,7 +448,7 @@
         )
 
     def start_over(self, i):
-        for k in range(self.across):
+        for k in range(self.across[i]):
             self.over_copy(i, k).start()
 
     def start_beside(self, i):
@@ -464,7 +475,7 @@
         def _():
             self.moved(i, a, 7, self.left).start()
 
-        if self.across == 1:
+        if self.across[i] == 1:
             self.moved(i, a, 10, self.side).start()
 
     def along(self, i, k):
@@ -501,9 +512,9 @@
 
     def complete(self, i):
         links = self.links
-        if self.across == 2:
+        if self.across[i] == 2:
             links.arrived(self.side_part(i, 0), self.flow(i, 1), self.over)
-        for k in range(self.across - 1, LINE):
+        for k in range(self.across[i] - 1, LINE):
             links.arrived(self.side_part(i, k), self.flow(i, 10 + k), self.side)
         self.pass_copy(i).start()
 
@@ -511,7 +522,7 @@
         links = self.links
         links.arrived(self.full[i].at[links.t ^ 1], self.flow(i, 2), self.sibling)
         links.arrived(self.full[i].at[self.last], self.flow(i, 3), self.sibling)
-        for k in range(self.across):
+        for k in range(self.across[i]):
             self.over_copy(i, k).wait_send()
         self.beside_copy(i).wait_send()
         self.stage_out(i).wait()
@@ -530,14 +541,14 @@
             def _():
                 self.moved(i, a + k, 7 + k, self.left).wait_send()
 
-        for k in range(self.across - 1, LINE):
+        for k in range(self.across[i] - 1, LINE):
             piece = a if k == 0 else jnp.where(k <= a, a - k, a + LINE - k)
             self.moved(i, piece, 10 + k, self.side).wait_send()
 
 
 class AdapterSpread(WeightGather):
     def __init__(self, links, base, full):
-        super().__init__(links, base, 1, None, full, None, None)
+        super().__init__(links, base, [1], None, full, None, None)
         self.half = lax.rem(links.t, 2)
 
     def part(self, i, a, b):
@@ -734,6 +745,16 @@
             self.over_copy(c).wait_send()
 
 
+def chunked(own, full, stage):
+    rows = own[-1].shape[0] // 2
+    halves = [pl.ds(o * rows, rows) for o in range(2)]
+    return (
+        list(own[:-1]) + [own[-1].at[at] for at in halves],
+        list(full[:-1]) + [full[-1].at[:, at] for at in halves],
+        list(stage[:-1]) + [stage[-1].at[at] for at in halves],
+    )
+
+
 def cut(refs, *counts):
     out, at = [], 0
     for count in counts:
@@ -742,36 +763,45 @@
     return out
 
 
-def self_forward_kernel(prefix_len, count, *refs):
-    ins, own, outs, full, stage, scratch = cut(refs, 10, count, 8, count, count + 1, 13)
-    x, memory, pre_cross, wq, wk, wv, wo, pre, seg_col, seg_row = ins
+def self_forward_kernel(prefix_len, arrays, *refs):
+    ins, own, outs, full, stage, scratch = cut(refs, 9, arrays, 8, arrays, arrays + 1, 14)
+    x, memory, pre_cross, wq, wk, wv, wo, pre, seg = ins
     q_out, k_out, v_out, a_out, l_out, resid, m_full, pre_full = outs
-    x_full, part, kept, bias, near, near_far, mid, far, send, recv, local, m_local, pre_local = scratch
+    x_full, part, kept, bias, near, near_far, mid, far, pre_stage, send, recv, local, m_local, pre_local = scratch
     links = Links(send, recv)
     t = links.t
     block, lanes = x.shape[0], q_out.shape[1]
-    weights = WeightGather(links, 0, 1, own, full, stage[:count], local)
+    own, full, held = chunked(own, full, stage[:arrays])
+    count = len(own)
+    weights = WeightGather(links, 0, [1] * (count - 2) + [2] * 2, own, full, held, local)
+    late = range(count - 2, count)
+    early = range(count - 2)
     at = count * FLOWS
     x_rows = RowGather(links, at, x, x_full)
     m_rows = RowGather(links, at + RowGather.FLOWS, memory, m_full)
     at += 2 * RowGather.FLOWS
     sums = RowScatter(links, at, part, near, near_far, mid, far)
     at += RowScatter.FLOWS
-    m_in = pltpu.make_async_copy(memory, stage[count], m_local.at[0])
-    m_keep = pltpu.make_async_copy(stage[count], m_full.at[t], m_local.at[1])
-    pre_keep = pltpu.make_async_copy(pre_cross, pre_full.at[t], pre_local.at[0])
+    m_in = pltpu.make_async_copy(memory, stage[arrays], m_local.at[0])
+    m_keep = pltpu.make_async_copy(stage[arrays], m_full.at[t], m_local.at[1])
+    pre_keep = pltpu.make_async_copy(pre_stage, pre_full.at[t], pre_local.at[0])
     pre_sends = [
-        links.copy(pre_cross, pre_full.at[t], at + m - 1, links.tp_peer(m)) for m in (1, 2, 3)
+        links.copy(pre_stage, pre_full.at[t], at + m - 1, links.tp_peer(m)) for m in (1, 2, 3)
     ]
 
-    kept[...] = jnp.zeros_like(kept)
     greet(
         [links.tp_peer(m) for m in (1, 2, 3)]
         + [links.line_peer(d) for d in range(1, LINE)]
         + [links.side_peer()]
     )
+    for i in early:
+        weights.start_over(i)
+    x_rows.start_beside()
     x_rows.start_over()
-    x_rows.start_beside()
+    kept[...] = jnp.zeros_like(kept)
+    pre_stage[...] = jnp.zeros_like(pre_stage)
+    for o in range(2):
+        pre_stage[o * PRE_PACK : o * PRE_PACK + prefix_len] = pre_cross[o]
     m_rows.start_beside()
     m_in.start()
     pre_keep.start()
@@ -780,9 +810,9 @@
     for i in range(count):
         weights.start_beside(i)
 
-    for target, at in ((k_out, 0), (v_out, PRE_PACK)):
-        target[0:PRE_PACK] = pre[at : at + PRE_PACK]
-        target[PRE_PACK:PRE] = jnp.zeros((PRE - PRE_PACK, lanes), bf16)
+    for target, o in ((k_out, 0), (v_out, 1)):
+        target[0:PRE] = jnp.zeros((PRE, lanes), bf16)
+        target[0:prefix_len] = pre[o]
 
     def project(rows, index):
         at = pl.multiple_of(index * block, block)
@@ -797,10 +827,13 @@
     m_keep.start()
     for i in range(count):
         weights.keep_own(i)
+    for i in early:
+        weights.came_over(i)
     x_rows.came_over()
-    for i in range(count):
+    for i in late:
         weights.start_over(i)
-    m_rows.start_over()
+    for i in early:
+        weights.along(i, 0)
     project(x_full[t ^ 2], t ^ 2)
     x_rows.came_last()
     project(x_full[t ^ 3], t ^ 3)
@@ -810,16 +843,16 @@
         here = t ^ (3 - order)
         for i in range(4):
             keys = PRE + (i + 1) * block
-            shape = (block, keys)
 
             @pl.when(here == i)
             def _():
-                bias[:, 0:keys] = mask_bias(
-                    seg_col[i * block : (i + 1) * block],
-                    seg_row[:, 0:keys],
-                    i * block + lax.broadcasted_iota(jnp.int32, shape, 0),
-                    lax.broadcasted_iota(jnp.int32, shape, 1),
-                    prefix_len,
+                bias[:, 0:PRE] = prefix_bias((block, PRE), 1, prefix_len)
+                bias[:, PRE:keys] = mask_bias(
+                    column(seg[:, i * block : (i + 1) * block]),
+                    seg[:, 0 : keys - PRE],
+                    (block, keys - PRE),
+                    1,
+                    i * block,
                 )
 
                 @pl.loop(0, lanes // PAIR)
@@ -840,31 +873,37 @@
         @pl.when(order == 0)
         def _():
             sums.first_copy().start()
-            for i in range(count):
-                weights.came_over(i)
+            for i in early:
+                weights.along(i, 1)
 
         @pl.when(order == 1)
         def _():
             sums.send_over()
+            m_rows.start_over()
+            for i in late:
+                weights.came_over(i)
 
         @pl.when(order == 2)
         def _():
             sums.second_copy().start()
-            for i in range(count):
-                weights.along(i, 0)
-
-    for i in range(count):
+            for i in early:
+                weights.along(i, 2)
+
+    for i in late:
+        weights.along(i, 0)
+    for i in early:
+        weights.complete(i)
+    for i in late:
         weights.along(i, 1)
-    m_rows.came_over()
-    for i in range(count):
-        weights.along(i, 2)
     sums.came_beside()
-    for i in range(count - 1):
-        weights.complete(i)
     for c in range(CHUNKS):
         rows = sums.at(c)
         resid[rows] = x[rows].astype(f32) + sums.came_over(c)
-    weights.complete(count - 1)
+    for i in late:
+        weights.along(i, 2)
+    m_rows.came_over()
+    for i in late:
+        weights.complete(i)
     m_rows.came_beside()
     m_rows.came_last()
     for m, one in zip((1, 2, 3), pre_sends):
@@ -885,9 +924,10 @@
     return count * FLOWS + 2 * RowGather.FLOWS + RowScatter.FLOWS
 
 
-def self_forward(prefix_len, x, memory, pre_cross, own_weights, pre, seg_col, seg_row, weights):
+def self_forward(prefix_len, x, memory, pre_cross, own_weights, pre, seg, weights):
     n = 4
-    count = len(weights)
+    arrays = len(weights)
+    count = arrays + 1
     block, width = x.shape
     lanes = own_weights[0].shape[1]
     seq = n * block
@@ -901,19 +941,19 @@
         out((n, 8, block), f32),
         out((block, width), f32),
         out((n, block, width), bf16),
-        out((n,) + pre_cross.shape, bf16),
+        out((n, 2 * PRE_PACK, lanes), bf16),
     ) + tuple(out((n,) + a.shape, a.dtype) for a in weights)
     a = pl.BlockSpec(memory_space=pltpu.HBM)
     rows = VMEM((block, width), bf16)
-    given = (x, memory, pre_cross, *own_weights, pre, seg_col, seg_row)
+    given = (x, memory, pre_cross, *own_weights, pre, seg)
     in_specs = [whole_spec(g.shape) for g in given]
     in_specs[1] = a
     return pl.pallas_call(
-        functools.partial(self_forward_kernel, prefix_len, count),
+        functools.partial(self_forward_kernel, prefix_len, arrays),
         grid=(1,),
         out_shape=outs,
-        in_specs=in_specs + [a] * count,
-        out_specs=[whole_spec(o.shape) for o in outs[:6]] + [a] * (2 + count),
+        in_specs=in_specs + [a] * arrays,
+        out_specs=[whole_spec(o.shape) for o in outs[:6]] + [a] * (2 + arrays),
         scratch_shapes=[VMEM(w.shape, w.dtype) for w in weights]
         + [rows]
         + [
@@ -925,6 +965,7 @@
             rows,
             rows,
             rows,
+            VMEM((2 * PRE_PACK, lanes), bf16),
             pltpu.SemaphoreType.DMA((flows,)),
             pltpu.SemaphoreType.DMA((flows,)),
             pltpu.SemaphoreType.DMA((2 * count,)),
@@ -932,7 +973,7 @@
             pltpu.SemaphoreType.DMA((1,)),
         ],
         compiler_params=pltpu.CompilerParams(
-            collective_id=0, has_side_effects=True, vmem_limit_bytes=48 << 20
+            collective_id=0, has_side_effects=True, vmem_limit_bytes=VMEM_BYTES
         ),
         name="self_forward",
     )(*given, *weights)
@@ -946,7 +987,7 @@
 
 
 def cross_backward_kernel(
-    prefix_len, levels, dr2, v1, q, k, v, a, logs, wq, wk, wv, wo, seg_row, seg_col, gain, vecs_in, g,
+    prefix_len, levels, dr2, v1, q, k, v, a, logs, wq, wk, wv, wo, dec, src, gain, vecs_in, g,
     dr1, dr1_full, dm, pre_grad, vecs, piece,
     dr1_low, dr2_low, bias, da, dq, dk, dv, total, s1, h, xb, h2, zb, p3, yb, hb, send, recv, local,
 ):
@@ -971,15 +1012,15 @@
         reduce.phase(0)
         dr2_low[...] = dr2[...].astype(bf16)
         total[...] = jnp.zeros_like(total)
-        bias[...] = mask_bias(
-            seg_row[...],
-            seg_col[...],
-            None,
-            lax.broadcasted_iota(jnp.int32, (keys, block), 0),
-            prefix_len,
-        )
+        own_queries = dec[:, pl.ds(pl.multiple_of(t * block, block), block)]
+        bias[0:PRE] = prefix_bias((PRE, block), 0, prefix_len)
+        bias[PRE:] = mask_bias(own_queries, column(src[...]), (keys - PRE, block), 0, None)
 
     da[...] = nt(dr2_low[...], wo[0]).astype(bf16)
+
+    @pl.when(step == 0)
+    def _():
+        reduce.phase(1)
 
     @pl.loop(0, lanes // PAIR)
     def _(j):
@@ -1000,11 +1041,10 @@
         dv[step, :, cols] = dv_pair[PRE:].astype(bf16)
 
     total[...] += nt(dq[...], wq[0])
-    for number in range(3):
-
-        @pl.when(step == number)
-        def _():
-            reduce.phase(number + 1)
+
+    @pl.when(step == 1)
+    def _():
+        reduce.phase(2)
 
     @pl.when(step == steps - 1)
     def _():
@@ -1020,7 +1060,7 @@
         vecs[...] = vecs_in[...]
         vecs[0:1] = gain_part
         vecs[3:4] = shift_part
-        piece[...] = reduce.result()
+        reduce.phase(3)
 
         @pl.loop(0, 4)
         def _(i):
@@ -1034,12 +1074,13 @@
         rows.came_over()
         rows.came_beside()
         rows.came_last()
+        piece[...] = reduce.result()
         rows.sent()
         keep.wait()
 
 
 def cross_backward(
-    prefix_len, row_count, dr2, v1, q, k, v, a, logs, weights, seg_row, seg_col, gain, vecs, grads
+    prefix_len, row_count, dr2, v1, q, k, v, a, logs, weights, dec, src, gain, vecs, grads
 ):
     wq, wk, wv, wo = weights
     n, block, lanes = q.shape
@@ -1069,7 +1110,7 @@
         in_specs=[whole_spec(dr2.shape), whole_spec(v1.shape)]
         + [shard_spec(x.shape) for x in (q, k, v, a, logs, wq)]
         + [whole_spec(wk.shape), whole_spec(wv.shape), shard_spec(wo.shape)]
-        + [whole_spec(x.shape) for x in (seg_row, seg_col, gain, vecs, g)],
+        + [whole_spec(x.shape) for x in (dec, src, gain, vecs, g)],
         out_specs=out_specs,
         scratch_shapes=[
             VMEM((block, width), bf16),
@@ -1093,10 +1134,10 @@
             pltpu.SemaphoreType.DMA((1,)),
         ],
         compiler_params=pltpu.CompilerParams(
-            collective_id=2, has_side_effects=True, vmem_limit_bytes=58 << 20
+            collective_id=2, has_side_effects=True, vmem_limit_bytes=VMEM_BYTES
         ),
         name="cross_backward",
-    )(dr2, v1, q, k, v, a, logs, wq, wk, wv, wo, seg_row, seg_col, gain, vecs, g)
+    )(dr2, v1, q, k, v, a, logs, wq, wk, wv, wo, dec, src, gain, vecs, g)
 
 
 class Doubling:
@@ -1127,7 +1168,7 @@
 
 
 def self_backward_kernel(
-    prefix_len, levels, dr1_full, dr1, q, k, v, a, logs, wq, wk, wv, wo, seg_row, seg_col,
+    prefix_len, levels, dr1_full, dr1, q, k, v, a, logs, wq, wk, wv, wo, seg,
     dm, piece, cross, vecs,
     tokens_grad, memory_grad, adapter, self_pre, sums,
     part, bias, da, dq, dk, dv, near, near_far, mid, far, m_near, m_near_far, m_mid, m_far,
@@ -1177,13 +1218,9 @@
     for i in reversed(range(4)):
         rows = slice(i * block, (i + 1) * block)
         keys = PRE + (i + 1) * block
-        shape = (keys, block)
-        bias[0:keys] = mask_bias(
-            seg_row[:, rows],
-            seg_col[0:keys],
-            i * block + lax.broadcasted_iota(jnp.int32, shape, 1),
-            lax.broadcasted_iota(jnp.int32, shape, 0),
-            prefix_len,
+        bias[0:PRE] = prefix_bias((PRE, block), 0, prefix_len)
+        bias[PRE:keys] = mask_bias(
+            seg[:, rows], column(seg[:, 0 : keys - PRE]), (keys - PRE, block), 0, i * block
         )
         da[...] = nt(dr1_full[i], wo[...]).astype(bf16)
 
@@ -1252,7 +1289,7 @@
 
 
 def self_backward(
-    prefix_len, row_count, dr1_full, dr1, q, k, v, a, logs, weights, seg_row, seg_col,
+    prefix_len, row_count, dr1_full, dr1, q, k, v, a, logs, weights, seg,
     dm, piece, cross, vecs,
 ):
     n, block, width = dr1_full.shape
@@ -1269,7 +1306,7 @@
         out((height, lanes), f32),
     )
     given = (
-        (dr1_full, dr1, q, k, v, a, logs) + tuple(weights) + (seg_row, seg_col, dm, piece, cross, vecs)
+        (dr1_full, dr1, q, k, v, a, logs) + tuple(weights) + (seg, dm, piece, cross, vecs)
     )
     rows = VMEM((block, width), bf16)
     flows = FLOWS + 2 * RowScatter.FLOWS + 2 * levels + 6
@@ -1301,10 +1338,70 @@
             pltpu.SemaphoreType.DMA((flows,)),
         ],
         compiler_params=pltpu.CompilerParams(
-            collective_id=3, has_side_effects=True, vmem_limit_bytes=58 << 20
+            collective_id=3, has_side_effects=True, vmem_limit_bytes=VMEM_BYTES
         ),
         name="self_backward",
     )(*given)
+
+
+def finish_kernel(
+    prefix_len, lanes, tokens_low, memory_low, adapter, self_pre, sums,
+    tokens_grad, memory_grad, self_out, cross_out, gains, shifts, down, down_bias, up, up_bias,
+):
+    tokens_grad[...] = tokens_low[...]
+    memory_grad[...] = memory_low[...]
+    up[...] = adapter[0].astype(f32)
+    down[...] = adapter[1].astype(f32).T
+
+    @pl.when(pl.program_id(0) == 0)
+    def _():
+        for o in range(2):
+            rows = slice(o * PRE_PACK, o * PRE_PACK + prefix_len)
+            self_out[o] = self_pre[rows]
+            cross_out[o] = sums[rows]
+        for i in range(gains.shape[1] // lanes):
+            at = 2 * PRE_PACK + 8 * i
+            cols = slice(i * lanes, (i + 1) * lanes)
+            gains[:, cols] = sums[at : at + 3]
+            shifts[:, cols] = sums[at + 3 : at + 6]
+            up_bias[:, cols] = sums[at + 6 : at + 7]
+            if (i + 1) * lanes <= down_bias.shape[1]:
+                down_bias[:, cols] = sums[at + 7 : at + 8]
+
+
+def finish(prefix_len, tokens_low, memory_low, adapter, self_pre, sums):
+    steps = 4
+    block, width = tokens_low.shape
+    adapt = adapter.shape[1]
+    lanes = sums.shape[1]
+    out = jax.ShapeDtypeStruct
+    outs = (
+        out((block, width), bf16),
+        out((block, width), bf16),
+        out((2, prefix_len, lanes), f32),
+        out((2, prefix_len, lanes), f32),
+        out((3, width), f32),
+        out((3, width), f32),
+        out((width, adapt), f32),
+        out((1, adapt), f32),
+        out((adapt, width), f32),
+        out((1, width), f32),
+    )
+    rows = pl.BlockSpec((block // steps, width), lambda i: (i, 0))
+    specs = [whole_spec(o.shape) for o in outs]
+    specs[0] = specs[1] = rows
+    specs[6] = pl.BlockSpec((width, adapt // steps), lambda i: (0, i))
+    specs[8] = pl.BlockSpec((adapt // steps, width), lambda i: (i, 0))
+    return pl.pallas_call(
+        functools.partial(finish_kernel, prefix_len, lanes),
+        grid=(steps,),
+        out_shape=outs,
+        in_specs=[rows, rows, pl.BlockSpec((2, adapt // steps, width), lambda i: (0, i, 0))]
+        + [whole_spec(self_pre.shape), whole_spec(sums.shape)],
+        out_specs=specs,
+        compiler_params=pltpu.CompilerParams(vmem_limit_bytes=VMEM_BYTES),
+        name="finish",
+    )(tokens_low, memory_low, adapter, self_pre, sums)
 
 
 def per_device(
@@ -1317,38 +1414,20 @@
 ):
     seq_local, _, width = tokens.shape
     prefix_len = self_prefix.shape[1]
-    lanes = self_query.shape[1]
     adapt = adapt_down.shape[1]
-    t = lax.axis_index("tp")
+    seq = dec_segments.shape[1]
     x, mem, grad_in = (a.reshape(seq_local, width) for a in (tokens, memory, out_grad))
-
-    def pack_prefix(prefix):
-        return jnp.pad(prefix, ((0, 0), (0, PRE_PACK - prefix_len), (0, 0))).reshape(
-            2 * PRE_PACK, lanes
-        )
-
-    def unpack_prefix(packed):
-        return packed.reshape(2, PRE_PACK, lanes)[:, :prefix_len]
-
-    seq = dec_segments.shape[1]
-    never = jnp.full((1, PRE), -1, jnp.int32)
-    dec_row = jnp.concatenate([never, dec_segments], axis=1)
-    src_row = jnp.concatenate([never, src_segments], axis=1)
-    dec_q = dec_segments
-    own_q = lax.dynamic_slice(dec_segments, (0, t * seq_local), (1, seq_local))
+    self_weights = (self_query, self_key, self_value, self_out)
 
     q1, k1, v1_heads, a1, logs1, resid_one, m_full, pre_full, *gathered = self_forward(
-        prefix_len, x, mem, pack_prefix(cross_prefix),
-        (self_query, self_key, self_value, self_out),
-        pack_prefix(self_prefix), dec_q.reshape(seq, 1), dec_row,
+        prefix_len, x, mem, cross_prefix, self_weights, self_prefix, dec_segments,
         (cross_query, cross_key, cross_value, cross_out, ffn_in),
     )
     cross_weights = gathered[:4]
     w_in = gathered[4]
-    m_full = m_full.reshape(seq, width)
     q2, k2, v2_heads, a2, logs2, resid_two, w_out = cross_forward(
-        prefix_len, resid_one, m_full, cross_weights, pre_full,
-        own_q.reshape(seq_local, 1), src_row, norm_gain, norm_shift, ffn_out,
+        prefix_len, resid_one, m_full.reshape(seq, width), cross_weights, pre_full,
+        dec_segments, src_segments, norm_gain, norm_shift, ffn_out,
     )
     output, dr2, grads, vecs = feed_forward(
         resid_two, grad_in, w_in, w_out,
@@ -1357,29 +1436,31 @@
     )
     dr1, dr1_full, dm, cross_pre_part, vecs, piece = cross_backward(
         prefix_len, row_count, dr2, resid_one, q2, k2, v2_heads, a2, logs2, cross_weights,
-        own_q, src_row.reshape(PRE + seq, 1), norm_gain, vecs, grads,
-    )
-    tokens_grad, memory_grad, adapter, self_pre, sums = self_backward(
+        dec_segments, src_segments, norm_gain, vecs, grads,
+    )
+    tokens_low, memory_low, adapter, self_pre, sums = self_backward(
         prefix_len, row_count, dr1_full, dr1, q1, k1, v1_heads, a1, logs1,
-        (self_query, self_key, self_value, self_out), dec_q, dec_row.reshape(PRE + seq, 1),
-        dm, piece, cross_pre_part, vecs,
-    )
-    adapter = adapter.reshape(2 * adapt, width)
-    cross_pre = sums[: 2 * PRE_PACK]
-    vecs = jnp.moveaxis(sums[2 * PRE_PACK :].reshape(-1, 8, lanes), 0, 1).reshape(8, width)
+        self_weights, dec_segments, dm, piece, cross_pre_part, vecs,
+    )
+    (
+        tokens_grad, memory_grad, self_grad, cross_grad, gains, shifts,
+        down, down_bias, up, up_bias,
+    ) = finish(
+        prefix_len, tokens_low, memory_low, adapter.reshape(2, adapt, width), self_pre, sums
+    )
     local = tokens.shape
     return (
         output.reshape(local),
         tokens_grad.reshape(local),
         memory_grad.reshape(local),
-        unpack_prefix(self_pre),
-        unpack_prefix(cross_pre),
-        vecs[0:3],
-        vecs[3:6],
-        adapter[adapt:].T.astype(f32),
-        vecs[7, :adapt],
-        adapter[:adapt].astype(f32),
-        vecs[6],
+        self_grad,
+        cross_grad,
+        gains,
+        shifts,
+        down,
+        down_bias.reshape(adapt),
+        up,
+        up_bias.reshape(width),
     )
 
 

time: 283 us -> 243 us (0.86)
  local copies, waits for them, and re-layouts: 30.9 us -> 5.77 us
  Pallas kernels: 249 us -> 236 us
    unnamed x54 -> x4, local copies, waits for them, and re-layouts: 21 us -> 5.77 us
    pallas_call x1, Pallas kernels: 55.3 us -> 49.7 us  [cross_backward(): pl.pallas_call(functools.partial(cross_backward_kernel, prefix_len, level...]
    pallas_call x1 -> x2, Pallas kernels: 79.7 us -> 74.6 us  [the longest x1 69.5 us: self_forward(): pl.pallas_call(functools.partial(self_forward_kernel, prefix_len, arrays)...]
    reshape x6 -> x0, local copies, waits for them, and re-layouts: 3.9 us -> none  [the longest x2 1.79 us: per_device(): src_row.reshape(PRE + seq, 1)]
    slice x6 -> x0, local copies, waits for them, and re-layouts: 3.57 us -> none  [the longest x1 1.77 us: per_device(): adapter[:adapt].astype(f32)]
    pallas_call x1, Pallas kernels: 48.6 us -> 45.8 us  [self_backward(): pl.pallas_call(functools.partial(self_backward_kernel, prefix_len, levels...]
where the time goes in v1:
time: 243 us; the launch traced here: 242 us
  Pallas kernels  236 us (97%)
  local copies, waits for them, and re-layouts  5.77 us (2%)
    pallas_call x1, Pallas kernels, self_forward(): pl.pallas_call(functools.partial(self_forward_kernel, prefix_len, arrays)...  69.5 us
    pallas_call x1, Pallas kernels, cross_backward(): pl.pallas_call(functools.partial(cross_backward_kernel, prefix_len, level...  49.7 us
    pallas_call x1, Pallas kernels, self_backward(): pl.pallas_call(functools.partial(self_backward_kernel, prefix_len, levels...  45.8 us
    pallas_call x1, Pallas kernels, cross_forward(): pl.pallas_call(functools.partial(cross_forward_kernel, prefix_len), grid=...  41.9 us
    pallas_call x1, Pallas kernels, feed_forward(): pl.pallas_call(feed_forward_kernel, grid=(2 * n,), out_shape=outs, in_spe...  23.9 us
    unnamed x4, local copies, waits for them, and re-layouts  5.77 us
    pallas_call x1, Pallas kernels, finish(): pl.pallas_call(functools.partial(finish_kernel, prefix_len, lanes), grid=...  5.07 us

profile of v1, /device:TPU:0, one launch (start us, length us, event | category | flops | bytes accessed | tf_op | source)
XLA Modules:
  0.0 242.3 jit_solution(14451893386331773129)
XLA Ops:
  0.6 1.4 copy.35.refs_7_
  2.0 1.4 copy.34.refs_2_
  3.4 69.5 %self_forward.1 = (bf16[1024,256]{1,0:T(8,128)(2,1)}, bf16[1152,256]{1,0:T(8,128)(2,1)}, bf16[1152,256]{1,0:T(8,128)(2,1)}, bf16[4,256,256]{2,1,0:T(8,128)(2,1)}...) custom-call(bf16[256,1024]{1,0:T(8,128)(2,1)} %bitcast.16, ...), custom_call_target="tpu_custom_call" | custom-call | tf_op jit(solution)/shard_map/self_forward/pallas_call | solution.py:951
  72.9 41.9 %cross_forward.1 = (bf16[4,256,256]{2,1,0:T(8,128)(2,1)}, bf16[4,1152,256]{2,1,0:T(8,128)(2,1)}, bf16[4,1152,256]{2,1,0:T(8,128)(2,1)}, bf16[4,256,256]{2,1,0:T(...) custom-call(f32[256,1024]{1,0:T(8,128)} %get-tuple-element.56.v1, ...), custom_call_target="tpu_custom_call" | custom-call | tf_op jit(solution)/shard_map/cross_forward/pallas_call | solution.py:226
  114.8 23.9 %feed_forward.1 = (bf16[256,1024]{1,0:T(8,128)(2,1)}, f32[256,1024]{1,0:T(8,128)}, bf16[2,512,1024]{2,1,0:T(8,128)(2,1)}, f32[8,1024]{1,0:T(8,128)}) custom-call(f32[256,1024]{1,0:T(8,128)} %get-tuple-element.63.v2, bf16[256,1024]{1,0:T(8,128)(2,1)} %bitcast.18, bf16[4,1024,1024]{2,1,0:T(8,128)(2,1)} %get-tuple-element.64.w_in, ...), custom_call_target="tpu_custom_call" | custom-call | tf_op jit(solution)/shard_map/feed_forward/pallas_call | solution.py:321
  138.7 49.7 %cross_backward.1 = (f32[256,1024]{1,0:T(8,128)}, bf16[4,256,1024]{2,1,0:T(8,128)(2,1)}, bf16[4,256,1024]{2,1,0:T(8,128)(2,1)}, f32[4,64,256]{2,1,0:T(8,128)}, f...) custom-call(f32[256,1024]{1,0:T(8,128)} %get-tuple-element.67.dr2, f32[256,1024]{1,0:T(8,128)} %get-tuple-element.56.v1, ...), custom_call_target="tpu_custom_call" | custom-call | tf_op jit(solution)/shard_map/cross_backward/pallas_call | solution.py:1106
  188.4 45.8 %self_backward.1 = (bf16[256,1024]{1,0:T(8,128)(2,1)}, bf16[256,1024]{1,0:T(8,128)(2,1)}, bf16[2,2,4,64,1024]{4,3,2,1,0:T(8,128)(2,1)}, f32[64,256]{1,0:T(8,128)}, f32[96,256]{1,0:T(8,128)}) custom-call(bf16[4,256,1024]{2,1,0:T(8,128)(2,1)} %get-tuple-element.75.dr1_full, f32[256,1024]{1,0:T(8,128)} %get-tuple-element.76.dr1, ...), custom_call_target="tpu_custom_call" | custom-call | tf_op jit(solution)/shard_map/self_backward/pallas_call | solution.py:1313
  234.2 5.1 %finish.1 = (bf16[256,1024]{1,0:T(8,128)(2,1)}, bf16[256,1024]{1,0:T(8,128)(2,1)}, f32[2,30,256]{2,1,0:T(8,128)}, f32[2,30,256]{2,1,0:T(8,128)}, f32[3,1024]{1,0...) custom-call(bf16[256,1024]{1,0:T(8,128)(2,1)} %get-tuple-element.86., ...), custom_call_target="tpu_custom_call" | custom-call | tf_op jit(solution)/shard_map/finish/pallas_call | solution.py:1395
  239.3 1.5 copy.36
  240.8 1.5 copy.37

commit v2 on v1

v2 whole, which is shorter than its diff:
```python
import functools

import jax
import jax.numpy as jnp
from jax import lax
from jax.experimental import pallas as pl
from jax.experimental.pallas import tpu as pltpu
from jax.sharding import PartitionSpec as P

HEAD = 64
PAIR = 2 * HEAD
PRE = 128
PRE_PACK = 32
GROUP = 8
LINE = 4
MASKED = -1000000000.0
EPSILON = 1e-05
VMEM_BYTES = 62 << 20
SCALE = HEAD**-0.5
f32 = jnp.float32
bf16 = jnp.bfloat16
MESH = pl.DeviceIdType.MESH
VMEM = pltpu.VMEM
ANY = pl.ANY


def nn(a, b):
    return lax.dot_general(a, b, (((1,), (0,)), ((), ())), preferred_element_type=f32)


def nt(a, b):
    return lax.dot_general(a, b, (((1,), (1,)), ((), ())), preferred_element_type=f32)


def tn(a, b):
    return lax.dot_general(a, b, (((0,), (0,)), ((), ())), preferred_element_type=f32)


def gelu_parts(v):
    phi = 0.5 + 0.5 * lax.erf(v * (0.5**0.5))
    slope = phi + v * (jnp.exp(-0.5 * v * v) * 0.3989422804014327)
    return v * phi, slope


def norm_parts(v):
    centered = v - jnp.mean(v, axis=-1, keepdims=True)
    spread = lax.rsqrt(jnp.mean(centered * centered, axis=-1, keepdims=True) + EPSILON)
    return centered * spread, spread


def norm_back(dy, gain, n, spread):
    dn = dy * gain
    dv = spread * (
        dn - jnp.mean(dn, axis=-1, keepdims=True) - n * jnp.mean(dn * n, axis=-1, keepdims=True)
    )
    return dv, jnp.sum(dy * n, axis=0, keepdims=True), jnp.sum(dy, axis=0, keepdims=True)


def lane_half(shape, h):
    return (lax.broadcasted_iota(jnp.int32, shape, 1) // HEAD) == h


def column(row):
    return jnp.broadcast_to(row, (8, row.shape[1])).T[:, 0:1]


def prefix_bias(shape, axis, prefix_len):
    return jnp.where(lax.broadcasted_iota(jnp.int32, shape, axis) < prefix_len, 0.0, MASKED)


def mask_bias(seg_q, seg_k, shape, key_axis, first_query):
    keep = seg_q == seg_k
    if first_query is not None:
        query = first_query + lax.broadcasted_iota(jnp.int32, shape, 1 - key_axis)
        keep = keep & (lax.broadcasted_iota(jnp.int32, shape, key_axis) <= query)
    return jnp.where(keep, 0.0, MASKED)


def pair_forward(q_pair, k_pair, v_pair, bias):
    outs, logs = [], []
    for h in range(2):
        half = lane_half(q_pair.shape, h)
        scores = nt(jnp.where(half, q_pair, jnp.zeros_like(q_pair)), k_pair) + bias
        top = jnp.max(scores, axis=1, keepdims=True)
        e = jnp.exp(scores - top)
        total = jnp.sum(e, axis=1, keepdims=True)
        outs.append(nn(e.astype(bf16), v_pair) * (1.0 / total))
        logs.append(top + jnp.log(total))
    return jnp.where(lane_half(outs[0].shape, 0), outs[0], outs[1]).astype(bf16), logs


def keep_logs(kept, logs, j):
    lane = lax.broadcasted_iota(jnp.int32, kept.shape, 1)
    for h in range(2):
        kept[...] = jnp.where(lane == 2 * j + h, logs[h], kept[...])


def pair_backward(q_pair, k_pair, v_pair, a_pair, da_pair, logs, bias_t):
    k_turned = k_pair.T
    prod = da_pair.astype(f32) * a_pair.astype(f32)
    prod_high = prod.astype(bf16)
    prod_low = (prod - prod_high.astype(f32)).astype(bf16)
    pick = (
        lax.broadcasted_iota(jnp.int32, (8, PAIR), 1) // HEAD
        == lax.broadcasted_iota(jnp.int32, (8, PAIR), 0)
    ).astype(bf16)
    delta = nt(pick, prod_high) + nt(pick, prod_low)
    dk = dv = None
    dq = []
    for h in range(2):
        half = lane_half(q_pair.shape, h)
        q = jnp.where(half, q_pair, jnp.zeros_like(q_pair))
        da = jnp.where(half, da_pair, jnp.zeros_like(da_pair))
        p = jnp.exp(nt(k_pair, q) + (bias_t - logs[h]))
        ds = (p * (nt(v_pair, da) - delta[h : h + 1])).astype(bf16)
        dv_h = nn(p.astype(bf16), da)
        dk_h = nn(ds, q)
        dk = dk_h if dk is None else dk + dk_h
        dv = dv_h if dv is None else dv + dv_h
        dq.append(nn(k_turned[h * HEAD : (h + 1) * HEAD], ds))
    return jnp.concatenate(dq, axis=0).T.astype(bf16), dk, dv


def whole_spec(shape):
    return pl.BlockSpec(shape, lambda i: (0,) * len(shape))


def shard_spec(shape, index=lambda i: i):
    return pl.BlockSpec((1,) + shape[1:], lambda i: (index(i), 0, 0))


def feed_forward_kernel(
    v2, out_grad, w_in, w_out, down, down_bias, up, up_bias, gain, shift,
    output, dr2, summed, vecs,
    n2_low, n2_hat, total, e_low, slope, grad, g, s1, h, xb, send, recv,
):
    step = pl.program_id(0)
    half = pl.num_programs(0) // 2
    links = Links(send, recv)
    reduce = AdapterReduce(links, 0, 0, g, s1, h, xb, summed, None, None, None, None)

    @pl.when(step == 0)
    def _():
        greet([links.tp_peer(1), links.side_peer()])
        n, _ = norm_parts(v2[...])
        n2_hat[...] = n
        normed = n * gain[1:2] + shift[1:2]
        total[...] = normed
        n2_low[...] = normed.astype(bf16)

    @pl.when(step < half)
    def _():
        act, bend = gelu_parts(nn(n2_low[...], w_in[0]))
        slope[step] = bend
        total[...] += nn(act.astype(bf16), w_out[0])

    @pl.when(step == half - 1)
    def _():
        act, bend = gelu_parts(nn(n2_low[...], down[...]) + down_bias[...])
        act = act.astype(bf16)
        resid = total[...] + 4.0 * (nn(act, up[...]) + up_bias[...])
        n, spread = norm_parts(resid)
        output[...] = (n * gain[2:3] + shift[2:3]).astype(bf16)
        dz, gain_part, shift_part = norm_back(out_grad[...].astype(f32), gain[2:3], n, spread)
        e_low[...] = dz.astype(bf16)
        four = (4.0 * dz).astype(bf16)
        g[0] = tn(act, four).astype(bf16).reshape(g.shape[1:])
        da = (nt(four, up[...]) * bend).astype(bf16)
        g[1] = tn(da, n2_low[...]).astype(bf16).reshape(g.shape[1:])
        reduce.start_beside()
        grad[...] = dz + nt(da, down[...])
        vecs[...] = jnp.zeros_like(vecs)
        vecs[2:3] = gain_part
        vecs[5:6] = shift_part
        vecs[6:7] = jnp.sum(four.astype(f32), axis=0, keepdims=True)
        vecs[7:8, 0 : down.shape[1]] = jnp.sum(da.astype(f32), axis=0, keepdims=True)

    @pl.when(step >= half)
    def _():
        du = (nt(e_low[...], w_out[0]) * slope[2 * half - 1 - step]).astype(bf16)
        grad[...] += nt(du, w_in[0])

    @pl.when(step == half)
    def _():
        reduce.start_side()

    @pl.when(step == 2 * half - 1)
    def _():
        _, spread = norm_parts(v2[...])
        dv, gain_part, shift_part = norm_back(grad[...], gain[1:2], n2_hat[...], spread)
        dr2[...] = dv
        vecs[1:2] = gain_part
        vecs[4:5] = shift_part
        reduce.sum_side()


def feed_forward(v2, out_grad, w_in, w_out, down, down_bias, up, up_bias, gain, shift):
    n, width, inner = w_in.shape
    block = v2.shape[0]
    adapt = down.shape[1]
    out = jax.ShapeDtypeStruct
    outs = (
        out((block, width), bf16),
        out((block, width), f32),
        out((LINE, adapt // GROUP, width), bf16),
        out((8, width), f32),
    )
    parts = (2, LINE, adapt // GROUP, width)
    turn = lambda i: jnp.minimum(i, 2 * n - 1 - i)
    return pl.pallas_call(
        feed_forward_kernel,
        grid=(2 * n,),
        out_shape=outs,
        in_specs=[whole_spec(v2.shape), whole_spec(out_grad.shape)]
        + [shard_spec(w_in.shape, turn), shard_spec(w_out.shape, turn)]
        + [whole_spec(a.shape) for a in (down, down_bias, up, up_bias, gain, shift)],
        out_specs=[whole_spec(a.shape) for a in outs],
        scratch_shapes=[
            VMEM((block, width), bf16),
            VMEM((block, width), f32),
            VMEM((block, width), f32),
            VMEM((block, width), bf16),
            VMEM((n, block, inner), f32),
            VMEM((block, width), f32),
            VMEM((2,) + parts, bf16),
            VMEM(parts, bf16),
            VMEM(parts, bf16),
            VMEM(parts[1:], bf16),
            pltpu.SemaphoreType.DMA((2,)),
            pltpu.SemaphoreType.DMA((2,)),
        ],
        compiler_params=pltpu.CompilerParams(
            collective_id=2, has_side_effects=True, vmem_limit_bytes=VMEM_BYTES
        ),
        name="feed_forward",
    )(v2, out_grad, w_in, w_out, down, down_bias, up, up_bias, gain, shift)


class Links:
    def __init__(self, send, recv):
        self.send, self.recv = send, recv
        self.row = lax.axis_index("rows")
        self.t = lax.axis_index("tp")
        self.flows = 0
        place = lax.rem(self.row, GROUP)
        self.base = self.row - place
        self.a = place // 2
        self.b = lax.rem(place, 2)
        self.place = place

    def flow(self):
        self.flows += 1
        return self.flows - 1

    def tp_peer(self, mask):
        return (self.row, self.t ^ mask)

    def line_peer(self, d):
        return (self.base + lax.rem(self.a + d, LINE) * 2 + self.b, self.t)

    def side_peer(self):
        return (self.base + self.a * 2 + (1 - self.b), self.t)

    def copy(self, src, dst, flow, peer):
        return pltpu.make_async_remote_copy(
            src_ref=src,
            dst_ref=dst,
            send_sem=self.send.at[flow],
            recv_sem=self.recv.at[flow],
            device_id=peer,
            device_id_type=MESH,
        )

    def start(self, src, dst, flow, peer):
        made = self.copy(src, dst, flow, peer)
        made.start()
        return made

    def arrived(self, dst, flow, peer):
        self.copy(dst, dst, flow, peer).wait_recv()


def greet(peers):
    barrier = pltpu.get_barrier_semaphore()
    for peer in peers:
        pl.semaphore_signal(barrier, inc=1, device_id=peer, device_id_type=MESH)
    pl.semaphore_wait(barrier, len(peers))


CHUNKS = 4


FLOWS = 14


class WeightGather:
    def __init__(self, links, base, across, own, full, stage, local):
        self.links, self.base, self.across = links, base, across
        self.own, self.full, self.stage, self.local = own, full, stage, local
        self.far, self.last = links.t ^ 2, links.t ^ 3
        a = links.a
        self.right = (links.base + jnp.minimum(a + 1, LINE - 1) * 2 + links.b, links.t)
        self.left = (links.base + jnp.maximum(a - 1, 0) * 2 + links.b, links.t)
        self.side = links.side_peer()
        self.sibling = links.tp_peer(1)
        self.over = links.tp_peer(2)

    def at(self, i, a, b):
        rows = self.own[i].shape[0] // GROUP
        return pl.ds(pl.multiple_of((a * 2 + b) * rows, rows), rows)

    def part(self, i, a, b):
        return self.full[i].at[self.far, self.at(i, a, b)]

    def flow(self, i, k):
        return self.base + i * FLOWS + k

    def over_copy(self, i, k):
        links = self.links
        b = links.b if k == 0 else 1 - links.b
        at = self.at(i, links.a, b)
        return links.copy(
            self.own[i].at[at], self.full[i].at[links.t, at], self.flow(i, k), self.over
        )

    def beside_copy(self, i):
        return self.links.copy(
            self.own[i], self.full[i].at[self.links.t], self.flow(i, 2), self.sibling
        )

    def pass_copy(self, i):
        whole = self.full[i].at[self.far]
        return self.links.copy(whole, whole, self.flow(i, 3), self.sibling)

    def moved(self, i, a, flow, peer):
        part = self.part(i, a, self.links.b)
        return self.links.copy(part, part, self.flow(i, flow), peer)

    def stage_in(self, i):
        stage = self.full[i].at[self.links.t] if self.stage is None else self.stage[i]
        return pltpu.make_async_copy(self.own[i], stage, self.local.at[2 * i])

    def stage_out(self, i):
        return pltpu.make_async_copy(
            self.stage[i], self.full[i].at[self.links.t], self.local.at[2 * i + 1]
        )

    def start_over(self, i, k):
        self.over_copy(i, k).start()

    def start_beside(self, i):
        self.beside_copy(i).start()
        self.stage_in(i).start()

    def own_ready(self, i):
        self.stage_in(i).wait()

    def beside_ready(self, i):
        self.links.arrived(self.full[i].at[self.links.t ^ 1], self.flow(i, 2), self.sibling)

    def far_ready(self, i):
        self.links.arrived(self.full[i].at[self.last], self.flow(i, 3), self.sibling)

    def keep_own(self, i):
        self.own_ready(i)
        self.stage_out(i).start()

    def came_over(self, i):
        mine = self.part(i, self.links.a, self.links.b)
        self.links.arrived(mine, self.flow(i, 0), self.over)
        self.spread(i)

    def spread(self, i):
        a = self.links.a

        @pl.when(a < LINE - 1)
        def _():
            self.moved(i, a, 4, self.right).start()

        @pl.when(a > 0)
        def _():
            self.moved(i, a, 7, self.left).start()

        if self.across[i] == 1:
            self.moved(i, a, 10, self.side).start()

    def along(self, i, k):
        links, a = self.links, self.links.a

        @pl.when(a - 1 - k >= 0)
        def _():
            links.arrived(self.part(i, a - 1 - k, links.b), self.flow(i, 4 + k), self.left)
            if k < LINE - 2:

                @pl.when(a < LINE - 1)
                def _():
                    self.moved(i, a - 1 - k, 5 + k, self.right).start()

            self.moved(i, a - 1 - k, 11 + k, self.side).start()

        @pl.when(a + 1 + k <= LINE - 1)
        def _():
            links.arrived(self.part(i, a + 1 + k, links.b), self.flow(i, 7 + k), self.right)
            if k < LINE - 2:

                @pl.when(a > 0)
                def _():
                    self.moved(i, a + 1 + k, 8 + k, self.left).start()

            self.moved(i, a + 1 + k, 13 - k, self.side).start()

    def side_part(self, i, k):
        links, a = self.links, self.links.a
        if k == 0:
            return self.part(i, a, 1 - links.b)
        piece = jnp.where(k <= a, a - k, a + LINE - k)
        return self.part(i, piece, 1 - links.b)

    def complete(self, i):
        links = self.links
        if self.across[i] == 2:
            links.arrived(self.side_part(i, 0), self.flow(i, 1), self.over)
        for k in range(self.across[i] - 1, LINE):
            links.arrived(self.side_part(i, k), self.flow(i, 10 + k), self.side)
        self.pass_copy(i).start()

    def finish(self, i):
        if self.stage is not None:
            self.beside_ready(i)
            self.far_ready(i)
            self.stage_out(i).wait()
        for k in range(self.across[i]):
            self.over_copy(i, k).wait_send()
        self.beside_copy(i).wait_send()
        self.spread_sent(i)

    def spread_sent(self, i):
        a = self.links.a
        self.pass_copy(i).wait_send()
        for k in range(LINE - 1):

            @pl.when((a < LINE - 1) & (a - k >= 0))
            def _():
                self.moved(i, a - k, 4 + k, self.right).wait_send()

            @pl.when((a > 0) & (a + k <= LINE - 1))
            def _():
                self.moved(i, a + k, 7 + k, self.left).wait_send()

        for k in range(self.across[i] - 1, LINE):
            piece = a if k == 0 else jnp.where(k <= a, a - k, a + LINE - k)
            self.moved(i, piece, 10 + k, self.side).wait_send()


class AdapterSpread(WeightGather):
    def __init__(self, links, base, full):
        super().__init__(links, base, [1], None, full, None, None)
        self.half = lax.rem(links.t, 2)

    def part(self, i, a, b):
        return self.full.at[self.half, b, a]

    def pass_copy(self, i):
        whole = self.full.at[self.half]
        return self.links.copy(whole, whole, self.flow(i, 3), self.sibling)

    def finish(self, i):
        self.links.arrived(self.full.at[1 - self.half], self.flow(i, 3), self.sibling)
        self.spread_sent(i)


class AdapterReduce:
    def __init__(self, links, base, levels, g, s1, h, xb, h2, zb, p3, yb, hb):
        self.links, self.base, self.levels = links, base, levels
        self.g, self.s1, self.h, self.xb, self.h2 = g, s1, h, xb, h2
        self.zb, self.p3, self.yb, self.hb = zb, p3, yb, hb
        self.half = lax.rem(links.t, 2)
        self.groups = [(links.row ^ (GROUP << level), links.t) for level in range(levels)]

    def beside(self):
        return self.links.copy(
            self.g.at[1 - self.half], self.s1, self.base, self.links.tp_peer(1)
        )

    def side(self):
        links = self.links
        return links.copy(self.h.at[1 - links.b], self.xb, self.base + 1, links.side_peer())

    def line(self, d):
        links = self.links
        return links.copy(
            self.h2.at[lax.rem(links.a + d, LINE)],
            self.zb.at[d - 1],
            self.base + 1 + d,
            links.line_peer(d),
        )

    def over(self):
        return self.links.copy(self.p3, self.yb, self.base + 1 + LINE, self.links.tp_peer(2))

    def group(self, level):
        return self.links.copy(
            self.hb.at[2 * level],
            self.hb.at[2 * level + 1],
            self.base + 2 + LINE + level,
            self.groups[level],
        )

    def start_beside(self):
        self.beside().start()

    def start_side(self):
        self.beside().wait()
        self.h[...] = (self.g[self.half].astype(f32) + self.s1[...].astype(f32)).astype(bf16)
        self.side().start()

    def sum_side(self):
        self.side().wait()
        self.h2[...] = (self.h[self.links.b].astype(f32) + self.xb[...].astype(f32)).astype(bf16)

    def start_line(self):
        for d in range(1, LINE):
            self.line(d).start()

    def start_over(self):
        for d in range(1, LINE):
            self.line(d).wait()
        total = self.h2[self.links.a].astype(f32)
        for d in range(1, LINE):
            total = total + self.zb[d - 1].astype(f32)
        self.p3[...] = total.astype(bf16)
        self.over().start()

    def result(self):
        self.over().wait()
        value = self.p3[...].astype(f32) + self.yb[...].astype(f32)
        for level in range(self.levels):
            self.hb[2 * level] = value.astype(bf16)
            self.group(level).start()
            self.group(level).wait()
            value = self.hb[2 * level].astype(f32) + self.hb[2 * level + 1].astype(f32)
        return value.astype(bf16)


class RowGather:
    FLOWS = 1 + 2 * 4

    def __init__(self, links, base, own, full):
        self.links, self.base, self.own, self.full = links, base, own, full
        self.far, self.last = links.t ^ 2, links.t ^ 3
        self.sibling, self.over = links.tp_peer(1), links.tp_peer(2)

    def at(self, c):
        rows = self.own.shape[0] // CHUNKS
        return pl.ds(c * rows, rows)

    def beside_copy(self):
        return self.links.copy(self.own, self.full.at[self.links.t], self.base, self.sibling)

    def over_copy(self, c):
        at = self.at(c)
        return self.links.copy(
            self.own.at[at], self.full.at[self.links.t, at], self.base + 1 + c, self.over
        )

    def pass_copy(self, c):
        part = self.full.at[self.far, self.at(c)]
        return self.links.copy(part, part, self.base + 1 + CHUNKS + c, self.sibling)

    def start_beside(self):
        self.beside_copy().start()

    def start_over(self):
        for c in range(CHUNKS):
            self.over_copy(c).start()

    def came_beside(self):
        self.links.arrived(self.full.at[self.links.t ^ 1], self.base, self.sibling)

    def came_over_chunk(self, c):
        self.links.arrived(self.full.at[self.far, self.at(c)], self.base + 1 + c, self.over)
        self.pass_copy(c).start()

    def came_over(self):
        for c in range(CHUNKS):
            self.came_over_chunk(c)

    def came_last(self):
        for c in range(CHUNKS):
            self.links.arrived(
                self.full.at[self.last, self.at(c)], self.base + 1 + CHUNKS + c, self.sibling
            )

    def sent(self):
        self.beside_copy().wait_send()
        for c in range(CHUNKS):
            self.over_copy(c).wait_send()
            self.pass_copy(c).wait_send()


class RowScatter:
    FLOWS = 2 + 4

    def __init__(self, links, base, part, near, near_far, mid, far):
        self.links, self.base, self.part = links, base, part
        self.near, self.near_far, self.mid, self.far = near, near_far, mid, far
        self.sibling, self.over = links.tp_peer(1), links.tp_peer(2)

    def at(self, c):
        rows = self.near.shape[0] // CHUNKS
        return pl.ds(c * rows, rows)

    def first_copy(self):
        return self.links.copy(
            self.part.at[self.links.t ^ 3], self.near_far, self.base, self.sibling
        )

    def second_copy(self):
        return self.links.copy(
            self.part.at[self.links.t ^ 1], self.near, self.base + 1, self.sibling
        )

    def over_copy(self, c):
        at = self.at(c)
        return self.links.copy(
            self.mid.at[at], self.far.at[at], self.base + 2 + c, self.over
        )

    def send_over(self):
        self.links.arrived(self.near_far, self.base, self.sibling)
        for c in range(CHUNKS):
            at = self.at(c)
            self.mid[at] = (
                self.part[self.links.t ^ 2, at].astype(f32) + self.near_far[at].astype(f32)
            ).astype(bf16)
            self.over_copy(c).start()

    def came_beside(self):
        self.links.arrived(self.near, self.base + 1, self.sibling)

    def came_over(self, c):
        at = self.at(c)
        self.links.arrived(self.far.at[at], self.base + 2 + c, self.over)
        return (
            self.part[self.links.t, at].astype(f32)
            + self.near[at].astype(f32)
            + self.far[at].astype(f32)
        )

    def sent(self):
        self.first_copy().wait_send()
        self.second_copy().wait_send()
        for c in range(CHUNKS):
            self.over_copy(c).wait_send()


def halves(own, full, stage):
    outs = ([], [], [])
    for one, whole, held in zip(own, full, stage):
        rows = one.shape[0] // 2
        for o in range(2):
            at = pl.ds(o * rows, rows)
            for out, view in zip(outs, (one.at[at], whole.at[:, at], held.at[at])):
                out.append(view)
    return outs


def cut(refs, *counts):
    out, at = [], 0
    for count in counts:
        out.append(refs[at : at + count])
        at += count
    return out


def forward_kernel(prefix_len, *refs):
    ins, self_outs, cross_outs, kept_outs, scratch = cut(refs, 18, 6, 6, 6, 26)
    x, pre_cross, wq, wk, wv, wo, pre, dec, src, gain, shift = ins[:11]
    memory, own_cross, own_ffn = ins[11], list(ins[12:16]), list(ins[16:18])
    q_out, k_out, v_out, a_out, l_out, resid = self_outs
    q2_out, k2_out, v2_out, a2_out, l2_out, resid2 = cross_outs
    cross_kept, ffn_full = list(kept_outs[:4]), list(kept_outs[4:])
    cross_full, held = list(scratch[:4]), list(scratch[4:6])
    (
        m_full, pre_full, x_full, part, kept, bias, near, near_far, mid, far, pre_stage, n1_low,
        send, recv, cross_local, ffn_local, m_local, keep_local, pre_local, spare,
    ) = scratch[6:]
    del spare
    block, lanes = x.shape[0], q_out.shape[1]
    links = Links(send, recv)
    t = links.t
    early = range(4)
    late = range(4)
    cross = WeightGather(links, 0, [1] * 4, own_cross, cross_full, None, cross_local)
    ffn = WeightGather(links, 4 * FLOWS, [2] * 4, *halves(own_ffn, ffn_full, held), ffn_local)
    at = 8 * FLOWS
    x_rows = RowGather(links, at, x, x_full)
    at += RowGather.FLOWS
    m_rows = RowGather(links, at, memory, m_full)
    at += RowGather.FLOWS
    sums = RowScatter(links, at, part, near, near_far, mid, far)
    at += RowScatter.FLOWS
    m_keep = pltpu.make_async_copy(memory, m_full.at[t], m_local.at[0])
    pre_keep = pltpu.make_async_copy(pre_stage, pre_full.at[t], pre_local.at[0])
    pre_sends = [
        links.copy(pre_stage, pre_full.at[t], at + m - 1, links.tp_peer(m)) for m in (1, 2, 3)
    ]
    cross_keeps = [
        pltpu.make_async_copy(cross_full[i], cross_kept[i], keep_local.at[i]) for i in range(4)
    ]

    greet(
        [links.tp_peer(m) for m in (1, 2, 3)]
        + [links.line_peer(d) for d in range(1, LINE)]
        + [links.side_peer()]
    )
    x_rows.start_over()
    x_rows.start_beside()
    kept[...] = jnp.zeros_like(kept)
    pre_stage[...] = jnp.zeros_like(pre_stage)
    for o in range(2):
        pre_stage[o * PRE_PACK : o * PRE_PACK + prefix_len] = pre_cross[:, o]
    pre_keep.start()
    for one in pre_sends:
        one.start()
    m_rows.start_beside()
    m_keep.start()
    for i in early:
        cross.start_beside(i)
    for i in late:
        ffn.start_beside(i)

    for target, o in ((k_out, 0), (v_out, 1)):
        target[0:PRE] = jnp.zeros((PRE, lanes), bf16)
        target[0:prefix_len] = pre[:, o]

    def project(rows, index):
        at = pl.multiple_of(index * block, block)
        q_out[pl.ds(at, block)] = (SCALE * nn(rows, wq[...])).astype(bf16)
        k_out[pl.ds(PRE + at, block)] = nn(rows, wk[...]).astype(bf16)
        v_out[pl.ds(PRE + at, block)] = nn(rows, wv[...]).astype(bf16)

    project(x[...], t)
    x_rows.came_beside()
    project(x_full[t ^ 1], t ^ 1)
    for c in range(CHUNKS):
        x_rows.came_over_chunk(c)
        if c == 1:
            for i in early:
                cross.start_over(i, 0)
    for i in range(2):
        ffn.start_over(i, 0)
    project(x_full[t ^ 2], t ^ 2)
    x_rows.came_last()
    project(x_full[t ^ 3], t ^ 3)

    @pl.loop(0, 4)
    def _(order):
        here = t ^ (3 - order)
        for i in range(4):
            keys = PRE + (i + 1) * block

            @pl.when(here == i)
            def _():
                bias[:, 0:PRE] = prefix_bias((block, PRE), 1, prefix_len)
                bias[:, PRE:keys] = mask_bias(
                    column(dec[:, i * block : (i + 1) * block]),
                    dec[:, 0 : keys - PRE],
                    (block, keys - PRE),
                    1,
                    i * block,
                )

                @pl.loop(0, lanes // PAIR)
                def _(j):
                    cols = pl.ds(pl.multiple_of(j * PAIR, PAIR), PAIR)
                    mixture, logs = pair_forward(
                        q_out[i * block : (i + 1) * block, cols],
                        k_out[0:keys, cols],
                        v_out[0:keys, cols],
                        bias[:, 0:keys],
                    )
                    a_out[i, :, cols] = mixture
                    keep_logs(kept, logs, j)

        l_out[here] = kept[...].T[0:8]
        part[here] = nn(a_out[here], wo[...]).astype(bf16)

        @pl.when(order == 0)
        def _():
            sums.first_copy().start()
            for i in early:
                cross.came_over(i)

        @pl.when(order == 1)
        def _():
            m_rows.start_over()
            sums.send_over()

        @pl.when(order == 2)
        def _():
            sums.second_copy().start()
            for i in early:
                cross.along(i, 0)

    for i in range(2):
        ffn.came_over(i)
    for i in late:
        ffn.keep_own(i)
    for i in early:
        cross.along(i, 1)
    for i in early:
        cross.along(i, 2)
    sums.came_beside()
    for c in range(CHUNKS):
        rows = sums.at(c)
        resid[rows] = x[rows].astype(f32) + sums.came_over(c)
    for i in range(2):
        ffn.start_over(i, 1)
    for k in range(2):
        for i in (2, 3):
            ffn.start_over(i, k)
    for i in range(2):
        ffn.along(i, 0)
    m_rows.came_over()

    n, _ = norm_parts(resid[...])
    normed = n * gain[0:1] + shift[0:1]
    resid2[...] = normed
    n1_low[...] = normed.astype(bf16)
    kept[...] = jnp.zeros_like(kept)
    own_queries = dec[:, pl.ds(pl.multiple_of(t * block, block), block)]
    keys = k2_out.shape[1]
    bias[:, 0:PRE] = prefix_bias((block, PRE), 1, prefix_len)
    bias[:, PRE:] = mask_bias(column(own_queries), src[...], (block, keys - PRE), 1, None)
    for i in early:
        cross.complete(i)
    m_rows.came_beside()
    m_rows.came_last()
    for m in (1, 2, 3):
        links.arrived(pre_full.at[t ^ m], at + m - 1, links.tp_peer(m))
    m_keep.wait()
    pre_keep.wait()
    for i in early:
        cross.own_ready(i)

    events = {
        0: [lambda: ffn.along(0, 1), lambda: ffn.along(1, 1)],
        2: [lambda: ffn.along(0, 2), lambda: ffn.came_over(2)],
        3: [lambda: ffn.along(1, 2), lambda: ffn.came_over(3)]
        + [functools.partial(cross.far_ready, i) for i in range(4)],
        4: [lambda: ffn.along(2, 0), lambda: ffn.complete(0)],
        5: [lambda: ffn.along(3, 0), lambda: ffn.along(2, 1), lambda: ffn.complete(1)],
        6: [lambda: ffn.along(3, 1), lambda: ffn.along(2, 2)],
        7: [lambda: ffn.along(3, 2)],
    }

    @pl.loop(0, 4)
    def _(order):
        s = t ^ order

        @pl.when(order == 1)
        def _():
            for i in early:
                cross.beside_ready(i)

        q2_out[s] = (SCALE * nn(n1_low[...], cross_full[0][s])).astype(bf16)
        for target, o in ((k2_out, 0), (v2_out, PRE_PACK)):
            target[s, 0:PRE_PACK] = pre_full[s, o : o + PRE_PACK]
            target[s, PRE_PACK:PRE] = jnp.zeros((PRE - PRE_PACK, lanes), bf16)

        @pl.loop(0, 4)
        def _(i):
            rows = m_full[i]
            to = pl.ds(pl.multiple_of(PRE + i * block, PRE), block)
            k2_out[s, to] = nn(rows, cross_full[1][s]).astype(bf16)
            v2_out[s, to] = nn(rows, cross_full[2][s]).astype(bf16)

        for j in range(lanes // PAIR):
            cols = slice(j * PAIR, (j + 1) * PAIR)
            mixture, logs = pair_forward(
                q2_out[s, :, cols], k2_out[s, :, cols], v2_out[s, :, cols], bias[...]
            )
            a2_out[s, :, cols] = mixture
            keep_logs(kept, logs, j)
            for step in range(4):

                @pl.when(order == step)
                def _():
                    for event in events.get(2 * step + j, []):
                        event()

        l2_out[s] = kept[...].T[0:8]
        resid2[...] += nn(a2_out[s], cross_full[3][s])

    for one in cross_keeps:
        one.start()
    for i in (2, 3):
        ffn.complete(i)
    for i in early:
        cross.finish(i)
    for i in late:
        ffn.finish(i)
    x_rows.sent()
    m_rows.sent()
    sums.sent()
    for one in pre_sends:
        one.wait_send()
    for one in cross_keeps:
        one.wait()


def forward(
    prefix_len, x, memory, prefixes, self_weights, cross_weights, ffn_weights, dec, src, gain, shift
):
    n = 4
    block, width = x.shape
    lanes = self_weights[0].shape[1]
    seq = n * block
    out = jax.ShapeDtypeStruct
    flows = 8 * FLOWS + 2 * RowGather.FLOWS + RowScatter.FLOWS + 3
    self_outs = (
        out((seq, lanes), bf16),
        out((PRE + seq, lanes), bf16),
        out((PRE + seq, lanes), bf16),
        out((n, block, lanes), bf16),
        out((n, 8, block), f32),
        out((block, width), f32),
    )
    cross_outs = (
        out((n, block, lanes), bf16),
        out((n, PRE + seq, lanes), bf16),
        out((n, PRE + seq, lanes), bf16),
        out((n, block, lanes), bf16),
        out((n, 8, block), f32),
        out((block, width), f32),
    )
    full = tuple(out((n,) + w.shape, w.dtype) for w in (*cross_weights, *ffn_weights))
    given = (x, prefixes[1], *self_weights, prefixes[0], dec, src, gain, shift)
    anywhere = pl.BlockSpec(memory_space=pltpu.HBM)
    rows = VMEM((block, width), bf16)
    all_rows = VMEM((n, block, width), bf16)
    dma = pltpu.SemaphoreType.DMA
    return pl.pallas_call(
        functools.partial(forward_kernel, prefix_len),
        grid=(1,),
        out_shape=self_outs + cross_outs + full,
        in_specs=[whole_spec(g.shape) for g in given] + [anywhere] * 7,
        out_specs=[whole_spec(o.shape) for o in self_outs + cross_outs] + [anywhere] * 6,
        scratch_shapes=[VMEM((n,) + w.shape, w.dtype) for w in cross_weights]
        + [VMEM(w.shape, w.dtype) for w in ffn_weights]
        + [
            all_rows,
            VMEM((n, 2 * PRE_PACK, lanes), bf16),
            all_rows,
            all_rows,
            VMEM((block, 128), f32),
            VMEM((block, PRE + seq), f32),
            rows,
            rows,
            rows,
            rows,
            VMEM((2 * PRE_PACK, lanes), bf16),
            rows,
            dma((flows,)),
            dma((flows,)),
            dma((8,)),
            dma((8,)),
            dma((1,)),
            dma((4,)),
            dma((1,)),
            dma((1,)),
        ],
        compiler_params=pltpu.CompilerParams(
            collective_id=0, has_side_effects=True, vmem_limit_bytes=VMEM_BYTES
        ),
        name="forward",
    )(*given, memory, *cross_weights, *ffn_weights)


def doublings(count):
    levels = 0
    while (1 << levels) < count:
        levels += 1
    return levels


class Doubling:
    def __init__(self, links, base, levels, outgo, income):
        self.links, self.base, self.levels = links, base, levels
        self.outgo, self.income = outgo, income

    def move(self, level):
        return self.links.copy(
            self.outgo.at[level],
            self.income.at[level],
            self.base + level,
            (self.links.row ^ (1 << level), self.links.t),
        )

    def begin(self, value):
        self.outgo[0] = value
        self.move(0).start()

    def value(self, level):
        self.move(level).wait()
        return self.outgo[level] + self.income[level]

    def step(self, level):
        value = self.value(level)
        self.outgo[level + 1] = value
        self.move(level + 1).start()


def backward_kernel(prefix_len, reduce_levels, levels, *refs):
    ins, later, outs, scratch = cut(refs, 16, 9, 5, 52)
    dr2, v1, q, k, v, a, logs, wq, wo, wk, wv, dec, src, gain, vecs_in, h2 = ins
    tokens_grad, memory_grad, adapter, self_pre, sums = outs
    (
        dr1, dr1_low, dr2_low, bias, da, dq, dk, dv, total, zb, p3, yb, hb,
        cross, vecs, dm, dr1_full, part, dq1, dk1, dv1,
        near, near_far, mid, far, m_near, m_near_far, m_mid, m_far,
        cross_beside, cross_mid, cross_over, vecs_beside, vecs_mid, vecs_over,
        outgo, income, pre_outgo, pre_income, send, recv, keep_sem, load_sem,
    ) = scratch[:-9]
    loaded = scratch[-9:]
    q1, k1, v1_heads, a1, logs1, wq1, wk1, wv1, wo1 = loaded
    step = pl.program_id(0)
    steps = pl.num_programs(0) - 1
    block, lanes = q.shape[1:]
    keys = k.shape[1]
    links = Links(send, recv)
    t = links.t
    at = 0
    rows = RowGather(links, at, dr1_low, dr1_full)
    at += RowGather.FLOWS
    reduce = AdapterReduce(links, at, reduce_levels, None, None, None, None, h2, zb, p3, yb, hb)
    at += 2 + LINE + reduce_levels
    spread = AdapterSpread(links, at, adapter)
    at += FLOWS
    m_sums = RowScatter(links, at, dm, m_near, m_near_far, m_mid, m_far)
    at += RowScatter.FLOWS
    x_sums = RowScatter(links, at, part, near, near_far, mid, far)
    at += RowScatter.FLOWS
    totals = Doubling(links, at, levels, outgo, income)
    at += levels
    pre_totals = Doubling(links, at, levels, pre_outgo, pre_income)
    at += levels
    keep = pltpu.make_async_copy(dr1_low, dr1_full.at[t], keep_sem.at[0])
    loads = [
        pltpu.make_async_copy(src_ref, dst_ref, load_sem.at[i])
        for i, (src_ref, dst_ref) in enumerate(zip(later, loaded))
    ]

    beside, over = links.tp_peer(1), links.tp_peer(2)
    to_beside = (
        links.copy(cross.at[t ^ 1], cross_beside.at[0], at, beside),
        links.copy(cross.at[t ^ 3], cross_beside.at[1], at + 1, beside),
        links.copy(vecs, vecs_beside, at + 2, beside),
    )
    to_over = (
        links.copy(cross_mid, cross_over, at + 3, over),
        links.copy(vecs_mid, vecs_over, at + 4, over),
    )

    @pl.when(step == 0)
    def _():
        greet(
            [links.tp_peer(m) for m in (1, 2, 3)]
            + [links.line_peer(d) for d in range(1, LINE)]
            + [links.side_peer()]
            + [(links.row ^ (1 << level), t) for level in range(doublings(GROUP), levels)]
        )
        reduce.start_line()
        dr2_low[...] = dr2[...].astype(bf16)
        total[...] = jnp.zeros_like(total)
        own_queries = dec[:, pl.ds(pl.multiple_of(t * block, block), block)]
        bias[0:PRE] = prefix_bias((PRE, block), 0, prefix_len)
        bias[PRE:] = mask_bias(own_queries, column(src[...]), (keys - PRE, block), 0, None)

    @pl.when(step < steps)
    def _():
        da[...] = nt(dr2_low[...], wo[0]).astype(bf16)

        @pl.when(step == 0)
        def _():
            for one in loads:
                one.start()

        @pl.loop(0, lanes // PAIR)
        def _(j):
            cols = pl.ds(pl.multiple_of(j * PAIR, PAIR), PAIR)
            dq_pair, dk_pair, dv_pair = pair_backward(
                q[0, :, cols],
                k[0, :, cols],
                v[0, :, cols],
                a[0, :, cols],
                da[:, cols],
                [logs[0, pl.ds(2 * j + i, 1)] for i in range(2)],
                bias[...],
            )
            dq[:, cols] = dq_pair
            cross[step, 0:PRE_PACK, cols] = dk_pair[0:PRE_PACK]
            cross[step, PRE_PACK : 2 * PRE_PACK, cols] = dv_pair[0:PRE_PACK]
            dk[step, :, cols] = dk_pair[PRE:].astype(bf16)
            dv[step, :, cols] = dv_pair[PRE:].astype(bf16)

            @pl.when((step == 2) & (j == 1))
            def _():
                reduce.start_over()

            @pl.when((step == 3) & (j == 1))
            def _():
                p3[...] = reduce.result()
                settle = pltpu.make_async_copy(
                    p3, adapter.at[spread.half, links.b, links.a], keep_sem.at[1]
                )
                settle.start()
                settle.wait()
                spread.spread(0)

        total[...] += nt(dq[...], wq[0])

    @pl.when(step == steps)
    def _():
        n, spread_one = norm_parts(v1[...])
        grad, gain_part, shift_part = norm_back(
            dr2[...] + SCALE * total[...], gain[0:1], n, spread_one
        )
        dr1_low[...] = grad.astype(bf16)
        rows.start_over()
        rows.start_beside()
        keep.start()
        dr1[...] = grad
        vecs[...] = vecs_in[...]
        vecs[0:1] = gain_part
        vecs[3:4] = shift_part
        for one in to_beside:
            one.start()
        dk1[...] = jnp.zeros_like(dk1)
        dv1[...] = jnp.zeros_like(dv1)

        @pl.loop(0, 4)
        def _(order):
            here = t ^ (3 - order)
            to = pl.ds(pl.multiple_of(here * block, block), block)
            value = None
            for shard in range(dk.shape[0]):
                term = nt(dk[shard, to], wk[shard]) + nt(dv[shard, to], wv[shard])
                value = term if value is None else value + term
            dm[here] = value.astype(bf16)

        m_sums.first_copy().start()
        m_sums.second_copy().start()
        for one in loads:
            one.wait()
        keep.wait()
        rows.came_beside()
        for one in to_beside:
            one.wait()
        cross_mid[...] = cross[t ^ 2] + cross_beside[1]
        vecs_mid[...] = vecs[...] + vecs_beside[...]
        for one in to_over:
            one.start()
        spread.along(0, 0)

        @pl.loop(0, 4)
        def _(order):
            here = t ^ order

            @pl.when(order == 2)
            def _():
                rows.came_over()
                m_sums.send_over()
                rows.came_last()

            da[...] = nt(dr1_full[here], wo1[...]).astype(bf16)
            for i in range(4):
                own = slice(i * block, (i + 1) * block)
                size = PRE + (i + 1) * block

                @pl.when(here == i)
                def _():
                    bias[0:PRE] = prefix_bias((PRE, block), 0, prefix_len)
                    bias[PRE:size] = mask_bias(
                        dec[:, own],
                        column(dec[:, 0 : size - PRE]),
                        (size - PRE, block),
                        0,
                        i * block,
                    )

                    @pl.loop(0, lanes // PAIR)
                    def _(j):
                        cols = pl.ds(pl.multiple_of(j * PAIR, PAIR), PAIR)
                        dq_pair, dk_pair, dv_pair = pair_backward(
                            q1[own, cols],
                            k1[0:size, cols],
                            v1_heads[0:size, cols],
                            a1[i, :, cols],
                            da[:, cols],
                            [logs1[i, pl.ds(2 * j + o, 1)] for o in range(2)],
                            bias[0:size],
                        )
                        dq1[i, :, cols] = dq_pair
                        dk1[0:size, cols] += dk_pair
                        dv1[0:size, cols] += dv_pair

            @pl.when(order < 2)
            def _():
                for k in range(2):

                    @pl.when(order == k)
                    def _():
                        spread.along(0, k + 1)

            @pl.when(order == 2)
            def _():
                for one in to_over:
                    one.wait()
                value = vecs_mid[...] + vecs_over[...]
                pieces = [cross[t] + cross_beside[0] + cross_over[...]] + [
                    value[:, o * lanes : (o + 1) * lanes] for o in range(vecs.shape[1] // lanes)
                ]
                totals.begin(jnp.concatenate(pieces, axis=0))
                spread.complete(0)

        pre_totals.begin(jnp.concatenate([dk1[0:PRE_PACK], dv1[0:PRE_PACK]], axis=0))
        for order in range(4):
            here = t ^ (3 - order)
            done = pl.ds(pl.multiple_of(PRE + here * block, PRE), block)
            part[here] = (
                SCALE * nt(dq1[here], wq1[...])
                + nt(dk1[done].astype(bf16), wk1[...])
                + nt(dv1[done].astype(bf16), wv1[...])
            ).astype(bf16)
            if order == 0:
                x_sums.first_copy().start()
                totals.step(0)
            if order == 1:
                x_sums.send_over()
                pre_totals.step(0)
            if order == 2:
                x_sums.second_copy().start()

        for level in range(1, levels - 1):
            totals.step(level)
            pre_totals.step(level)
        m_sums.came_beside()
        for c in range(CHUNKS):
            memory_grad[m_sums.at(c)] = m_sums.came_over(c).astype(bf16)
        sums[...] = totals.value(levels - 1)
        self_pre[...] = pre_totals.value(levels - 1)
        x_sums.came_beside()
        for c in range(CHUNKS):
            here = x_sums.at(c)
            tokens_grad[here] = (dr1[here] + x_sums.came_over(c)).astype(bf16)
        spread.finish(0)
        rows.sent()
        m_sums.sent()
        x_sums.sent()


def backward(
    prefix_len, row_count, dr2, resid_one, cross_saved, cross_weights, self_saved, self_weights,
    dec, src, gain, vecs, summed,
):
    q, k, v, a, logs = cross_saved
    wq, wk, wv, wo = cross_weights
    n, block, lanes = q.shape
    keys = k.shape[1]
    width = dr2.shape[1]
    reduce_levels = doublings(row_count // GROUP)
    levels = doublings(row_count)
    piece = summed.shape[1]
    half = (2, LINE, piece, width)
    packed = 2 * PRE_PACK
    height = packed + vecs.shape[0] * width // lanes
    out = jax.ShapeDtypeStruct
    outs = (
        out((block, width), bf16),
        out((block, width), bf16),
        out((2,) + half, bf16),
        out((packed, lanes), f32),
        out((height, lanes), f32),
    )
    flows = (
        RowGather.FLOWS + 2 + LINE + reduce_levels + FLOWS + 2 * RowScatter.FLOWS + 2 * levels + 5
    )
    later = (*self_saved, *self_weights)
    low, wide = VMEM((block, width), bf16), VMEM((block, width), f32)
    dma = pltpu.SemaphoreType.DMA
    bounded = lambda i: jnp.minimum(i, n - 1)

    def once(x):
        return pl.BlockSpec(x.shape, lambda i: (0,) * len(x.shape), pipeline_mode=pl.Buffered(1))

    return pl.pallas_call(
        functools.partial(backward_kernel, prefix_len, reduce_levels, levels),
        grid=(n + 1,),
        out_shape=outs,
        in_specs=[once(dr2), once(resid_one)]
        + [shard_spec(x.shape, bounded) for x in (q, k, v, a, logs, wq, wo)]
        + [once(x) for x in (wk, wv, dec, src, gain, vecs, summed)]
        + [pl.BlockSpec(memory_space=pltpu.HBM)] * len(later),
        out_specs=[whole_spec(o.shape) for o in outs[:2]]
        + [pl.BlockSpec(memory_space=pltpu.HBM)]
        + [whole_spec(o.shape) for o in outs[3:]],
        scratch_shapes=[
            wide,
            low,
            low,
            VMEM((keys, block), f32),
            VMEM((block, lanes), bf16),
            VMEM((block, lanes), bf16),
            VMEM((n, keys - PRE, lanes), bf16),
            VMEM((n, keys - PRE, lanes), bf16),
            wide,
            VMEM((LINE - 1, piece, width), bf16),
            VMEM((piece, width), bf16),
            VMEM((piece, width), bf16),
            VMEM((max(1, 2 * reduce_levels), piece, width), bf16),
            VMEM((n, packed, lanes), f32),
            VMEM(vecs.shape, f32),
            VMEM((n, block, width), bf16),
            VMEM((n, block, width), bf16),
            VMEM((n, block, width), bf16),
            VMEM((n, block, lanes), bf16),
            VMEM((keys, lanes), f32),
            VMEM((keys, lanes), f32),
        ]
        + [low] * 8
        + [
            VMEM((2, packed, lanes), f32),
            VMEM((packed, lanes), f32),
            VMEM((packed, lanes), f32),
            VMEM(vecs.shape, f32),
            VMEM(vecs.shape, f32),
            VMEM(vecs.shape, f32),
            VMEM((levels, height, lanes), f32),
            VMEM((levels, height, lanes), f32),
            VMEM((levels, packed, lanes), f32),
            VMEM((levels, packed, lanes), f32),
            dma((flows,)),
            dma((flows,)),
            dma((2,)),
            dma((len(later),)),
        ]
        + [VMEM(x.shape, x.dtype) for x in later],
        compiler_params=pltpu.CompilerParams(
            collective_id=1, has_side_effects=True, vmem_limit_bytes=VMEM_BYTES
        ),
        name="backward",
    )(dr2, resid_one, q, k, v, a, logs, wq, wo, wk, wv, dec, src, gain, vecs, summed, *later)


def finish_kernel(
    prefix_len, lanes, output_low, tokens_low, memory_low, adapter, self_pre, sums,
    output, tokens_grad, memory_grad, self_out, cross_out, gains, shifts, down, down_bias, up, up_bias,
):
    output[...] = output_low[...]
    tokens_grad[...] = tokens_low[...]
    memory_grad[...] = memory_low[...]
    up[...] = adapter[0].astype(f32)
    down[...] = adapter[1].astype(f32).T

    @pl.when(pl.program_id(0) == 0)
    def _():
        for o in range(2):
            rows = slice(o * PRE_PACK, o * PRE_PACK + prefix_len)
            self_out[:, o] = self_pre[rows]
            cross_out[:, o] = sums[rows]
        for i in range(gains.shape[1] // lanes):
            at = 2 * PRE_PACK + 8 * i
            cols = slice(i * lanes, (i + 1) * lanes)
            gains[:, cols] = sums[at : at + 3]
            shifts[:, cols] = sums[at + 3 : at + 6]
            up_bias[:, cols] = sums[at + 6 : at + 7]
            if (i + 1) * lanes <= down_bias.shape[1]:
                down_bias[:, cols] = sums[at + 7 : at + 8]


def finish(prefix_len, output_low, tokens_low, memory_low, adapter, self_pre, sums):
    steps = 4
    block, width = tokens_low.shape
    adapt = adapter.shape[1]
    lanes = sums.shape[1]
    out = jax.ShapeDtypeStruct
    outs = (
        out((block, width), bf16),
        out((block, width), bf16),
        out((block, width), bf16),
        out((prefix_len, 2, lanes), f32),
        out((prefix_len, 2, lanes), f32),
        out((3, width), f32),
        out((3, width), f32),
        out((width, adapt), f32),
        out((1, adapt), f32),
        out((adapt, width), f32),
        out((1, width), f32),
    )
    rows = pl.BlockSpec((block // steps, width), lambda i: (i, 0))
    specs = [whole_spec(o.shape) for o in outs]
    specs[0] = specs[1] = specs[2] = rows
    specs[7] = pl.BlockSpec((width, adapt // steps), lambda i: (0, i))
    specs[9] = pl.BlockSpec((adapt // steps, width), lambda i: (i, 0))
    return pl.pallas_call(
        functools.partial(finish_kernel, prefix_len, lanes),
        grid=(steps,),
        out_shape=outs,
        in_specs=[rows, rows, rows, pl.BlockSpec((2, adapt // steps, width), lambda i: (0, i, 0))]
        + [whole_spec(self_pre.shape), whole_spec(sums.shape)],
        out_specs=specs,
        compiler_params=pltpu.CompilerParams(vmem_limit_bytes=VMEM_BYTES),
        name="finish",
    )(output_low, tokens_low, memory_low, adapter, self_pre, sums)


def per_device(
    row_count,
    tokens, memory, out_grad, dec_segments, src_segments,
    self_query, self_key, self_value, self_out,
    cross_query, cross_key, cross_value, cross_out,
    ffn_in, ffn_out, adapt_down, adapt_down_bias, adapt_up, adapt_up_bias,
    self_prefix, cross_prefix, norm_gain, norm_shift,
):
    seq_local, _, width = tokens.shape
    prefix_len = self_prefix.shape[1]
    adapt = adapt_down.shape[1]
    x, mem, grad_in = (a.reshape(seq_local, width) for a in (tokens, memory, out_grad))
    self_weights = (self_query, self_key, self_value, self_out)

    (
        q1, k1, v1_heads, a1, logs1, resid_one, q2, k2, v2_heads, a2, logs2, resid_two, *gathered
    ) = forward(
        prefix_len, x, mem, [jnp.swapaxes(p, 0, 1) for p in (self_prefix, cross_prefix)], self_weights,
        (cross_query, cross_key, cross_value, cross_out), (ffn_in, ffn_out),
        dec_segments, src_segments, norm_gain, norm_shift,
    )
    cross_weights, (w_in, w_out) = gathered[:4], gathered[4:]
    output_low, dr2, summed, vecs = feed_forward(
        resid_two, grad_in, w_in, w_out,
        adapt_down, adapt_down_bias.reshape(1, adapt), adapt_up, adapt_up_bias.reshape(1, width),
        norm_gain, norm_shift,
    )
    tokens_low, memory_low, adapter, self_pre, sums = backward(
        prefix_len, row_count, dr2, resid_one, (q2, k2, v2_heads, a2, logs2), cross_weights,
        (q1, k1, v1_heads, a1, logs1), self_weights,
        dec_segments, src_segments, norm_gain, vecs, summed,
    )
    (
        output, tokens_grad, memory_grad, self_grad, cross_grad, gains, shifts,
        down, down_bias, up, up_bias,
    ) = finish(
        prefix_len, output_low, tokens_low, memory_low, adapter.reshape(2, adapt, width), self_pre, sums
    )
    local = tokens.shape
    return (
        output.reshape(local),
        tokens_grad.reshape(local),
        memory_grad.reshape(local),
        jnp.swapaxes(self_grad, 0, 1),
        jnp.swapaxes(cross_grad, 0, 1),
        gains,
        shifts,
        down,
        down_bias.reshape(adapt),
        up,
        up_bias.reshape(width),
    )


def solution(mesh):
    placed = (
        (P("tp", "rows", None),) * 3
        + (P("rows", None),) * 2
        + (P(None, "tp"),) * 3
        + (P("tp", None),)
        + (P(None, "tp"),) * 3
        + (P("tp", None),)
        + (P(None, "tp"), P("tp", None))
        + (P(),) * 4
        + (P(None, None, "tp"),) * 2
        + (P(),) * 2
    )
    return jax.shard_map(
        functools.partial(per_device, mesh.shape["rows"]),
        mesh=mesh,
        in_specs=placed,
        out_specs=(P("tp", "rows", None),) * 3 + (P(None, None, "tp"),) * 2 + (P(),) * 6,
        check_vma=False,
    )
```

time: 243 us -> 204 us (0.84)
  Pallas kernels: 236 us -> 203 us
  local copies, waits for them, and re-layouts: 5.77 us -> 0 us
    pallas_call x4 -> x2, Pallas kernels: 207 us -> 166 us  [the longest x1 101 us: forward(): pl.pallas_call(functools.partial(forward_kernel, prefix_len), grid=(1,),...]
    pallas_call x1, Pallas kernels: 23.9 us -> 32.2 us  [feed_forward(): pl.pallas_call(feed_forward_kernel, grid=(2 * n,), out_shape=outs, in_spe...]
    unnamed x4 -> x0, local copies, waits for them, and re-layouts: 5.77 us -> none
where the time goes in v2:
time: 204 us
  Pallas kernels  203 us (100%)
    pallas_call x1, Pallas kernels, forward(): pl.pallas_call(functools.partial(forward_kernel, prefix_len), grid=(1,),...  101 us
    pallas_call x1, Pallas kernels, backward(): pl.pallas_call(functools.partial(backward_kernel, prefix_len, reduce_leve...  64.8 us
    pallas_call x1, Pallas kernels, feed_forward(): pl.pallas_call(feed_forward_kernel, grid=(2 * n,), out_shape=outs, in_spe...  32.2 us
    pallas_call x1, Pallas kernels, finish(): pl.pallas_call(functools.partial(finish_kernel, prefix_len, lanes), grid=...  5.42 us

profile of v2, /device:TPU:0, one launch (start us, length us, event | category | flops | bytes accessed | tf_op | source)
XLA Modules:
  0.0 204.2 jit_solution(406101736753768448)
XLA Ops:
  0.6 101.0 %forward.1 = (bf16[1024,256]{1,0:T(8,128)(2,1)}, bf16[1152,256]{1,0:T(8,128)(2,1)}, bf16[1152,256]{1,0:T(8,128)(2,1)}, bf16[4,256,256]{2,1,0:T(8,128)(2,1)}, f32...) custom-call(bf16[256,1024]{1,0:T(8,128)(2,1)} %bitcast.16, ...), custom_call_target="tpu_custom_call" | custom-call | tf_op jit(solution)/shard_map/forward/pallas_call | solution.py:944
  101.7 32.2 %feed_forward.1 = (bf16[256,1024]{1,0:T(8,128)(2,1)}, f32[256,1024]{1,0:T(8,128)}, bf16[4,64,1024]{2,1,0:T(8,128)(2,1)}, f32[8,1024]{1,0:T(8,128)}) custom-call(f32[256,1024]{1,0:T(8,128)} %get-tuple-element.49.v2, bf16[256,1024]{1,0:T(8,128)(2,1)} %bitcast.18, bf16[4,1024,1024]{2,1,0:T(8,128)(2,1)} %get-tuple-element.50.w_in, ...), custom_call_target="tpu_custom_call" | custom-call | tf_op jit(solution)/shard_map/feed_forward/pallas_call | solution.py:210
  133.8 64.8 %backward.1 = (bf16[256,1024]{1,0:T(8,128)(2,1)}, bf16[256,1024]{1,0:T(8,128)(2,1)}, bf16[2,2,4,64,1024]{4,3,2,1,0:T(8,128)(2,1)}, f32[64,256]{1,0:T(8,128)}, f32[96,256]{1,0:T(8,128)}) custom-call(f32[256,1024]{1,0:T(8,128)} %get-tuple-element.53.refs_0_, f32[256,1024]{1,0:T(8,128)} %get-tuple-element.54.refs_1_, ...), custom_call_target="tpu_custom_call" | custom-call | tf_op jit(solution)/shard_map/backward/pallas_call | solution.py:1298
  198.6 5.4 %finish.1 = (bf16[256,1024]{1,0:T(8,128)(2,1)}, bf16[256,1024]{1,0:T(8,128)(2,1)}, bf16[256,1024]{1,0:T(8,128)(2,1)}, f32[30,2,256]{2,1,0:T(2,128)}, f32[30,2,25...) custom-call(bf16[256,1024]{1,0:T(8,128)(2,1)} %get-tuple-element.52., ...), custom_call_target="tpu_custom_call" | custom-call | tf_op jit(solution)/shard_map/finish/pallas_call | solution.py:1407

commit v3 on v2

--- a/solution.py
+++ b/solution.py
@@ -131,13 +131,13 @@
 
 def feed_forward_kernel(
     v2, out_grad, w_in, w_out, down, down_bias, up, up_bias, gain, shift,
-    output, dr2, summed, vecs,
+    output, dr2, summed, rest, vecs,
     n2_low, n2_hat, total, e_low, slope, grad, g, s1, h, xb, send, recv,
 ):
     step = pl.program_id(0)
     half = pl.num_programs(0) // 2
     links = Links(send, recv)
-    reduce = AdapterReduce(links, 0, 0, g, s1, h, xb, summed, None, None, None, None)
+    reduce = AdapterReduceFirst(links, g, s1, h, xb)
 
     @pl.when(step == 0)
     def _():
@@ -191,7 +191,7 @@
         dr2[...] = dv
         vecs[1:2] = gain_part
         vecs[4:5] = shift_part
-        reduce.sum_side()
+        reduce.finish(summed, rest)
 
 
 def feed_forward(v2, out_grad, w_in, w_out, down, down_bias, up, up_bias, gain, shift):
@@ -203,6 +203,7 @@
         out((block, width), bf16),
         out((block, width), f32),
         out((LINE, adapt // GROUP, width), bf16),
+        out((LINE // 2, adapt // GROUP, width), bf16),
         out((8, width), f32),
     )
     parts = (2, LINE, adapt // GROUP, width)
@@ -225,7 +226,7 @@
             VMEM((2,) + parts, bf16),
             VMEM(parts, bf16),
             VMEM(parts, bf16),
-            VMEM(parts[1:], bf16),
+            VMEM((LINE // 2,) + parts[2:], bf16),
             pltpu.SemaphoreType.DMA((2,)),
             pltpu.SemaphoreType.DMA((2,)),
         ],
@@ -469,58 +470,86 @@
         self.spread_sent(i)
 
 
+class AdapterReduceFirst:
+    def __init__(self, links, g, s1, h, xb):
+        self.links, self.g, self.s1, self.h, self.xb = links, g, s1, h, xb
+        self.half = lax.rem(links.t, 2)
+
+    def beside(self):
+        return self.links.copy(self.g.at[1 - self.half], self.s1, 0, self.links.tp_peer(1))
+
+    def side(self):
+        links = self.links
+        return links.copy(
+            self.h.at[1 - links.b, pl.ds(0, LINE // 2)], self.xb, 1, links.side_peer()
+        )
+
+    def start_beside(self):
+        self.beside().start()
+
+    def start_side(self):
+        self.beside().wait()
+        self.h[...] = (self.g[self.half].astype(f32) + self.s1[...].astype(f32)).astype(bf16)
+        self.side().start()
+
+    def finish(self, summed, rest):
+        kept = LINE // 2
+        mine = self.h[self.links.b]
+        rest[...] = self.h[1 - self.links.b, kept:]
+        summed[kept:] = mine[kept:]
+        self.side().wait()
+        summed[0:kept] = (mine[0:kept].astype(f32) + self.xb[...].astype(f32)).astype(bf16)
+
+
 class AdapterReduce:
-    def __init__(self, links, base, levels, g, s1, h, xb, h2, zb, p3, yb, hb):
+    def __init__(self, links, base, levels, summed, rest, xb, h2, zb, p3, yb, hb):
         self.links, self.base, self.levels = links, base, levels
-        self.g, self.s1, self.h, self.xb, self.h2 = g, s1, h, xb, h2
+        self.summed, self.rest, self.xb, self.h2 = summed, rest, xb, h2
         self.zb, self.p3, self.yb, self.hb = zb, p3, yb, hb
         self.half = lax.rem(links.t, 2)
         self.groups = [(links.row ^ (GROUP << level), links.t) for level in range(levels)]
 
-    def beside(self):
+    def side(self):
+        return self.links.copy(self.rest, self.xb, self.base, self.links.side_peer())
+
+    def piece(self, d):
+        return lax.rem(self.links.a + d, LINE)
+
+    def line(self, d):
         return self.links.copy(
-            self.g.at[1 - self.half], self.s1, self.base, self.links.tp_peer(1)
+            self.h2.at[self.piece(d)], self.zb.at[d - 1], self.base + d, self.links.line_peer(d)
         )
 
-    def side(self):
-        links = self.links
-        return links.copy(self.h.at[1 - links.b], self.xb, self.base + 1, links.side_peer())
-
-    def line(self, d):
-        links = self.links
-        return links.copy(
-            self.h2.at[lax.rem(links.a + d, LINE)],
-            self.zb.at[d - 1],
-            self.base + 1 + d,
-            links.line_peer(d),
-        )
-
     def over(self):
-        return self.links.copy(self.p3, self.yb, self.base + 1 + LINE, self.links.tp_peer(2))
+        return self.links.copy(self.p3, self.yb, self.base + LINE, self.links.tp_peer(2))
 
     def group(self, level):
         return self.links.copy(
             self.hb.at[2 * level],
             self.hb.at[2 * level + 1],
-            self.base + 2 + LINE + level,
+            self.base + LINE + 1 + level,
             self.groups[level],
         )
 
-    def start_beside(self):
-        self.beside().start()
-
-    def start_side(self):
-        self.beside().wait()
-        self.h[...] = (self.g[self.half].astype(f32) + self.s1[...].astype(f32)).astype(bf16)
+    def start(self):
+        kept = LINE // 2
         self.side().start()
-
-    def sum_side(self):
+        self.h2[0:kept] = self.summed[0:kept]
+        for d in range(1, LINE):
+
+            @pl.when(self.piece(d) < kept)
+            def _():
+                self.line(d).start()
+
+    def start_line(self):
+        kept = LINE // 2
         self.side().wait()
-        self.h2[...] = (self.h[self.links.b].astype(f32) + self.xb[...].astype(f32)).astype(bf16)
-
-    def start_line(self):
+        self.h2[kept:] = (self.summed[kept:].astype(f32) + self.xb[...].astype(f32)).astype(bf16)
         for d in range(1, LINE):
-            self.line(d).start()
+
+            @pl.when(self.piece(d) >= kept)
+            def _():
+                self.line(d).start()
 
     def start_over(self):
         for d in range(1, LINE):
@@ -723,12 +752,7 @@
     pre_keep.start()
     for one in pre_sends:
         one.start()
-    m_rows.start_beside()
     m_keep.start()
-    for i in early:
-        cross.start_beside(i)
-    for i in late:
-        ffn.start_beside(i)
 
     for target, o in ((k_out, 0), (v_out, 1)):
         target[0:PRE] = jnp.zeros((PRE, lanes), bf16)
@@ -745,13 +769,14 @@
     project(x_full[t ^ 1], t ^ 1)
     for c in range(CHUNKS):
         x_rows.came_over_chunk(c)
-        if c == 1:
+        if c == 3:
             for i in early:
                 cross.start_over(i, 0)
-    for i in range(2):
-        ffn.start_over(i, 0)
     project(x_full[t ^ 2], t ^ 2)
     x_rows.came_last()
+    for i in early:
+        cross.start_beside(i)
+    m_rows.start_beside()
     project(x_full[t ^ 3], t ^ 3)
 
     @pl.loop(0, 4)
@@ -791,10 +816,11 @@
             sums.first_copy().start()
             for i in early:
                 cross.came_over(i)
+            for i in range(2):
+                ffn.start_over(i, 0)
 
         @pl.when(order == 1)
         def _():
-            m_rows.start_over()
             sums.send_over()
 
         @pl.when(order == 2)
@@ -806,23 +832,16 @@
     for i in range(2):
         ffn.came_over(i)
     for i in late:
-        ffn.keep_own(i)
+        ffn.start_beside(i)
     for i in early:
         cross.along(i, 1)
-    for i in early:
-        cross.along(i, 2)
+    for i in range(2):
+        ffn.along(i, 0)
     sums.came_beside()
     for c in range(CHUNKS):
         rows = sums.at(c)
         resid[rows] = x[rows].astype(f32) + sums.came_over(c)
-    for i in range(2):
-        ffn.start_over(i, 1)
-    for k in range(2):
-        for i in (2, 3):
-            ffn.start_over(i, k)
-    for i in range(2):
-        ffn.along(i, 0)
-    m_rows.came_over()
+    m_rows.start_over()
 
     n, _ = norm_parts(resid[...])
     normed = n * gain[0:1] + shift[0:1]
@@ -834,7 +853,12 @@
     bias[:, 0:PRE] = prefix_bias((block, PRE), 1, prefix_len)
     bias[:, PRE:] = mask_bias(column(own_queries), src[...], (block, keys - PRE), 1, None)
     for i in early:
-        cross.complete(i)
+        cross.along(i, 2)
+    for i in range(2):
+        ffn.along(i, 1)
+    m_rows.came_over()
+    for i in (2, 3):
+        ffn.start_over(i, 0)
     m_rows.came_beside()
     m_rows.came_last()
     for m in (1, 2, 3):
@@ -844,15 +868,22 @@
     for i in early:
         cross.own_ready(i)
 
+    def each(method, indices, *more):
+        def run():
+            for i in indices:
+                method(i, *more)
+
+        return run
+
     events = {
-        0: [lambda: ffn.along(0, 1), lambda: ffn.along(1, 1)],
-        2: [lambda: ffn.along(0, 2), lambda: ffn.came_over(2)],
-        3: [lambda: ffn.along(1, 2), lambda: ffn.came_over(3)]
-        + [functools.partial(cross.far_ready, i) for i in range(4)],
-        4: [lambda: ffn.along(2, 0), lambda: ffn.complete(0)],
-        5: [lambda: ffn.along(3, 0), lambda: ffn.along(2, 1), lambda: ffn.complete(1)],
-        6: [lambda: ffn.along(3, 1), lambda: ffn.along(2, 2)],
-        7: [lambda: ffn.along(3, 2)],
+        0: [each(ffn.keep_own, late), each(ffn.along, (0, 1), 2)],
+        1: [each(ffn.came_over, (2,)), each(cross.complete, early)],
+        2: [each(ffn.came_over, (3,)), each(ffn.start_over, late, 1)],
+        3: [each(ffn.along, (2,), 0), each(cross.far_ready, early)],
+        4: [each(ffn.along, (3,), 0), each(ffn.along, (2,), 1)],
+        5: [each(ffn.along, (3,), 1)],
+        6: [each(ffn.along, (2,), 2), each(ffn.complete, (0, 1))],
+        7: [each(ffn.along, (3,), 2)],
     }
 
     @pl.loop(0, 4)
@@ -1013,11 +1044,11 @@
 
 
 def backward_kernel(prefix_len, reduce_levels, levels, *refs):
-    ins, later, outs, scratch = cut(refs, 16, 9, 5, 52)
-    dr2, v1, q, k, v, a, logs, wq, wo, wk, wv, dec, src, gain, vecs_in, h2 = ins
+    ins, later, outs, scratch = cut(refs, 17, 9, 5, 54)
+    dr2, v1, q, k, v, a, logs, wq, wo, wk, wv, dec, src, gain, vecs_in, summed, rest = ins
     tokens_grad, memory_grad, adapter, self_pre, sums = outs
     (
-        dr1, dr1_low, dr2_low, bias, da, dq, dk, dv, total, zb, p3, yb, hb,
+        dr1, dr1_low, dr2_low, bias, da, dq, dk, dv, total, xb, h2, zb, p3, yb, hb,
         cross, vecs, dm, dr1_full, part, dq1, dk1, dv1,
         near, near_far, mid, far, m_near, m_near_far, m_mid, m_far,
         cross_beside, cross_mid, cross_over, vecs_beside, vecs_mid, vecs_over,
@@ -1034,8 +1065,8 @@
     at = 0
     rows = RowGather(links, at, dr1_low, dr1_full)
     at += RowGather.FLOWS
-    reduce = AdapterReduce(links, at, reduce_levels, None, None, None, None, h2, zb, p3, yb, hb)
-    at += 2 + LINE + reduce_levels
+    reduce = AdapterReduce(links, at, reduce_levels, summed, rest, xb, h2, zb, p3, yb, hb)
+    at += 1 + LINE + reduce_levels
     spread = AdapterSpread(links, at, adapter)
     at += FLOWS
     m_sums = RowScatter(links, at, dm, m_near, m_near_far, m_mid, m_far)
@@ -1071,7 +1102,7 @@
             + [links.side_peer()]
             + [(links.row ^ (1 << level), t) for level in range(doublings(GROUP), levels)]
         )
-        reduce.start_line()
+        reduce.start()
         dr2_low[...] = dr2[...].astype(bf16)
         total[...] = jnp.zeros_like(total)
         own_queries = dec[:, pl.ds(pl.multiple_of(t * block, block), block)]
@@ -1105,19 +1136,14 @@
             dk[step, :, cols] = dk_pair[PRE:].astype(bf16)
             dv[step, :, cols] = dv_pair[PRE:].astype(bf16)
 
-            @pl.when((step == 2) & (j == 1))
+            @pl.when((step == 1) & (j == 1))
+            def _():
+                reduce.start_line()
+
+            @pl.when((step == 3) & (j == 1))
             def _():
                 reduce.start_over()
 
-            @pl.when((step == 3) & (j == 1))
-            def _():
-                p3[...] = reduce.result()
-                settle = pltpu.make_async_copy(
-                    p3, adapter.at[spread.half, links.b, links.a], keep_sem.at[1]
-                )
-                settle.start()
-                settle.wait()
-                spread.spread(0)
 
         total[...] += nt(dq[...], wq[0])
 
@@ -1162,7 +1188,13 @@
         vecs_mid[...] = vecs[...] + vecs_beside[...]
         for one in to_over:
             one.start()
-        spread.along(0, 0)
+        p3[...] = reduce.result()
+        settle = pltpu.make_async_copy(
+            p3, adapter.at[spread.half, links.b, links.a], keep_sem.at[1]
+        )
+        settle.start()
+        settle.wait()
+        spread.spread(0)
 
         @pl.loop(0, 4)
         def _(order):
@@ -1206,13 +1238,11 @@
                         dk1[0:size, cols] += dk_pair
                         dv1[0:size, cols] += dv_pair
 
-            @pl.when(order < 2)
-            def _():
-                for k in range(2):
-
-                    @pl.when(order == k)
-                    def _():
-                        spread.along(0, k + 1)
+            for k in range(3):
+
+                @pl.when(order == k)
+                def _():
+                    spread.along(0, k)
 
             @pl.when(order == 2)
             def _():
@@ -1223,7 +1253,6 @@
                     value[:, o * lanes : (o + 1) * lanes] for o in range(vecs.shape[1] // lanes)
                 ]
                 totals.begin(jnp.concatenate(pieces, axis=0))
-                spread.complete(0)
 
         pre_totals.begin(jnp.concatenate([dk1[0:PRE_PACK], dv1[0:PRE_PACK]], axis=0))
         for order in range(4):
@@ -1246,6 +1275,7 @@
         for level in range(1, levels - 1):
             totals.step(level)
             pre_totals.step(level)
+        spread.complete(0)
         m_sums.came_beside()
         for c in range(CHUNKS):
             memory_grad[m_sums.at(c)] = m_sums.came_over(c).astype(bf16)
@@ -1263,7 +1293,7 @@
 
 def backward(
     prefix_len, row_count, dr2, resid_one, cross_saved, cross_weights, self_saved, self_weights,
-    dec, src, gain, vecs, summed,
+    dec, src, gain, vecs, summed, rest,
 ):
     q, k, v, a, logs = cross_saved
     wq, wk, wv, wo = cross_weights
@@ -1285,7 +1315,7 @@
         out((height, lanes), f32),
     )
     flows = (
-        RowGather.FLOWS + 2 + LINE + reduce_levels + FLOWS + 2 * RowScatter.FLOWS + 2 * levels + 5
+        RowGather.FLOWS + 1 + LINE + reduce_levels + FLOWS + 2 * RowScatter.FLOWS + 2 * levels + 5
     )
     later = (*self_saved, *self_weights)
     low, wide = VMEM((block, width), bf16), VMEM((block, width), f32)
@@ -1301,7 +1331,7 @@
         out_shape=outs,
         in_specs=[once(dr2), once(resid_one)]
         + [shard_spec(x.shape, bounded) for x in (q, k, v, a, logs, wq, wo)]
-        + [once(x) for x in (wk, wv, dec, src, gain, vecs, summed)]
+        + [once(x) for x in (wk, wv, dec, src, gain, vecs, summed, rest)]
         + [pl.BlockSpec(memory_space=pltpu.HBM)] * len(later),
         out_specs=[whole_spec(o.shape) for o in outs[:2]]
         + [pl.BlockSpec(memory_space=pltpu.HBM)]
@@ -1316,6 +1346,8 @@
             VMEM((n, keys - PRE, lanes), bf16),
             VMEM((n, keys - PRE, lanes), bf16),
             wide,
+            VMEM((LINE // 2, piece, width), bf16),
+            VMEM((LINE, piece, width), bf16),
             VMEM((LINE - 1, piece, width), bf16),
             VMEM((piece, width), bf16),
             VMEM((piece, width), bf16),
@@ -1351,18 +1383,20 @@
             collective_id=1, has_side_effects=True, vmem_limit_bytes=VMEM_BYTES
         ),
         name="backward",
-    )(dr2, resid_one, q, k, v, a, logs, wq, wo, wk, wv, dec, src, gain, vecs, summed, *later)
+    )(dr2, resid_one, q, k, v, a, logs, wq, wo, wk, wv, dec, src, gain, vecs, summed, rest, *later)
 
 
 def finish_kernel(
-    prefix_len, lanes, output_low, tokens_low, memory_low, adapter, self_pre, sums,
+    prefix_len, lanes, output_low, tokens_low, memory_low, up_low, down_low, self_pre, sums,
     output, tokens_grad, memory_grad, self_out, cross_out, gains, shifts, down, down_bias, up, up_bias,
 ):
     output[...] = output_low[...]
     tokens_grad[...] = tokens_low[...]
     memory_grad[...] = memory_low[...]
-    up[...] = adapter[0].astype(f32)
-    down[...] = adapter[1].astype(f32).T
+    up[...] = up_low[0].astype(f32)
+    rows = down.shape[0]
+    at = pl.multiple_of(pl.program_id(0) * rows, rows)
+    down[...] = down_low[0, :, pl.ds(at, rows)].astype(f32).T
 
     @pl.when(pl.program_id(0) == 0)
     def _():
@@ -1402,18 +1436,20 @@
     rows = pl.BlockSpec((block // steps, width), lambda i: (i, 0))
     specs = [whole_spec(o.shape) for o in outs]
     specs[0] = specs[1] = specs[2] = rows
-    specs[7] = pl.BlockSpec((width, adapt // steps), lambda i: (0, i))
+    specs[7] = pl.BlockSpec((width // steps, adapt), lambda i: (i, 0))
     specs[9] = pl.BlockSpec((adapt // steps, width), lambda i: (i, 0))
     return pl.pallas_call(
         functools.partial(finish_kernel, prefix_len, lanes),
         grid=(steps,),
         out_shape=outs,
-        in_specs=[rows, rows, rows, pl.BlockSpec((2, adapt // steps, width), lambda i: (0, i, 0))]
+        in_specs=[rows, rows, rows]
+        + [pl.BlockSpec((1, adapt // steps, width), lambda i: (0, i, 0))]
+        + [pl.BlockSpec((1, adapt, width), lambda i: (1, 0, 0))]
         + [whole_spec(self_pre.shape), whole_spec(sums.shape)],
         out_specs=specs,
         compiler_params=pltpu.CompilerParams(vmem_limit_bytes=VMEM_BYTES),
         name="finish",
-    )(output_low, tokens_low, memory_low, adapter, self_pre, sums)
+    )(output_low, tokens_low, memory_low, adapter, adapter, self_pre, sums)
 
 
 def per_device(
@@ -1438,7 +1474,7 @@
         dec_segments, src_segments, norm_gain, norm_shift,
     )
     cross_weights, (w_in, w_out) = gathered[:4], gathered[4:]
-    output_low, dr2, summed, vecs = feed_forward(
+    output_low, dr2, summed, rest, vecs = feed_forward(
         resid_two, grad_in, w_in, w_out,
         adapt_down, adapt_down_bias.reshape(1, adapt), adapt_up, adapt_up_bias.reshape(1, width),
         norm_gain, norm_shift,
@@ -1446,7 +1482,7 @@
     tokens_low, memory_low, adapter, self_pre, sums = backward(
         prefix_len, row_count, dr2, resid_one, (q2, k2, v2_heads, a2, logs2), cross_weights,
         (q1, k1, v1_heads, a1, logs1), self_weights,
-        dec_segments, src_segments, norm_gain, vecs, summed,
+        dec_segments, src_segments, norm_gain, vecs, summed, rest,
     )
     (
         output, tokens_grad, memory_grad, self_grad, cross_grad, gains, shifts,

time: 204 us -> 201 us (0.985)
  Pallas kernels: 203 us -> 200 us
    pallas_call x1, Pallas kernels: 32.2 us -> 26.6 us  [feed_forward(): pl.pallas_call(feed_forward_kernel, grid=(2 * n,), out_shape=outs, in_spe...]
    pallas_call x1, Pallas kernels: 64.8 us -> 68.2 us  [backward(): pl.pallas_call(functools.partial(backward_kernel, prefix_len, reduce_leve...]
where the time goes in v3:
time: 201 us
  Pallas kernels  200 us (100%)
    pallas_call x1, Pallas kernels, forward(): pl.pallas_call(functools.partial(forward_kernel, prefix_len), grid=(1,),...  99.4 us
    pallas_call x1, Pallas kernels, backward(): pl.pallas_call(functools.partial(backward_kernel, prefix_len, reduce_leve...  68.2 us
    pallas_call x1, Pallas kernels, feed_forward(): pl.pallas_call(feed_forward_kernel, grid=(2 * n,), out_shape=outs, in_spe...  26.6 us
    pallas_call x1, Pallas kernels, finish(): pl.pallas_call(functools.partial(finish_kernel, prefix_len, lanes), grid=...  5.56 us

profile of v3, /device:TPU:0, one launch (start us, length us, event | category | flops | bytes accessed | tf_op | source)
XLA Modules:
  0.0 200.6 jit_solution(1301063579930233096)
XLA Ops:
  0.6 99.4 %forward.1 = (bf16[1024,256]{1,0:T(8,128)(2,1)}, bf16[1152,256]{1,0:T(8,128)(2,1)}, bf16[1152,256]{1,0:T(8,128)(2,1)}, bf16[4,256,256]{2,1,0:T(8,128)(2,1)}, f32...) custom-call(bf16[256,1024]{1,0:T(8,128)(2,1)} %bitcast.17, ...), custom_call_target="tpu_custom_call" | custom-call | tf_op jit(solution)/shard_map/forward/pallas_call | solution.py:975
  100.0 26.6 %feed_forward.1 = (bf16[256,1024]{1,0:T(8,128)(2,1)}, f32[256,1024]{1,0:T(8,128)}, bf16[4,64,1024]{2,1,0:T(8,128)(2,1)}, bf16[2,64,1024]{2,1,0:T(8,128)(2,1)}, f32[8,1024]{1,0:T(8,128)}) custom-call(f32[256,1024]{1,0:T(8,128)} %get-tuple-element.50.v2, bf16[256,1024]{1,0:T(8,128)(2,1)} %bitcast.19, bf16[4,1024,1024]{2,1,0:T(8,128)(2,1)} %get-tuple-element.51.w_in, ...), custom_call_target="tpu_custom_call" | custom-call | tf_op jit(solution)/shard_map/feed_forward/pallas_call | solution.py:211
  126.6 68.2 %backward.1 = (bf16[256,1024]{1,0:T(8,128)(2,1)}, bf16[256,1024]{1,0:T(8,128)(2,1)}, bf16[2,2,4,64,1024]{4,3,2,1,0:T(8,128)(2,1)}, f32[64,256]{1,0:T(8,128)}, f32[96,256]{1,0:T(8,128)}) custom-call(f32[256,1024]{1,0:T(8,128)} %get-tuple-element.54.refs_0_, f32[256,1024]{1,0:T(8,128)} %get-tuple-element.55.refs_1_, ...), custom_call_target="tpu_custom_call" | custom-call | tf_op jit(solution)/shard_map/backward/pallas_call | solution.py:1328
  194.9 5.6 %finish.1 = (bf16[256,1024]{1,0:T(8,128)(2,1)}, bf16[256,1024]{1,0:T(8,128)(2,1)}, bf16[256,1024]{1,0:T(8,128)(2,1)}, f32[30,2,256]{2,1,0:T(2,128)}, f32[30,2,25...) custom-call(bf16[256,1024]{1,0:T(8,128)(2,1)} %get-tuple-element.53., ...), custom_call_target="tpu_custom_call" | custom-call | tf_op jit(solution)/shard_map/finish/pallas_call | solution.py:1441

commit v4 on v3

--- a/solution.py
+++ b/solution.py
@@ -826,6 +826,7 @@
         @pl.when(order == 2)
         def _():
             sums.second_copy().start()
+            m_rows.start_over()
             for i in early:
                 cross.along(i, 0)
 
@@ -841,8 +842,6 @@
     for c in range(CHUNKS):
         rows = sums.at(c)
         resid[rows] = x[rows].astype(f32) + sums.came_over(c)
-    m_rows.start_over()
-
     n, _ = norm_parts(resid[...])
     normed = n * gain[0:1] + shift[0:1]
     resid2[...] = normed
@@ -1415,7 +1414,7 @@
 
 
 def finish(prefix_len, output_low, tokens_low, memory_low, adapter, self_pre, sums):
-    steps = 4
+    steps = 2
     block, width = tokens_low.shape
     adapt = adapter.shape[1]
     lanes = sums.shape[1]

time: 201 us -> 200 us (level)
  no operation moved by 1% of the time
where the time goes in v4:
time: 200 us; the launch traced here: 199 us
  Pallas kernels  199 us (100%)
    pallas_call x1, Pallas kernels, forward(): pl.pallas_call(functools.partial(forward_kernel, prefix_len), grid=(1,),...  99.2 us
    pallas_call x1, Pallas kernels, backward(): pl.pallas_call(functools.partial(backward_kernel, prefix_len, reduce_leve...  68.1 us
    pallas_call x1, Pallas kernels, feed_forward(): pl.pallas_call(feed_forward_kernel, grid=(2 * n,), out_shape=outs, in_spe...  26.6 us
    pallas_call x1, Pallas kernels, finish(): pl.pallas_call(functools.partial(finish_kernel, prefix_len, lanes), grid=...  4.67 us

profile of v4, /device:TPU:0, one launch (start us, length us, event | category | flops | bytes accessed | tf_op | source)
XLA Modules:
  0.0 199.4 jit_solution(3440497832854173858)
XLA Ops:
  0.6 99.2 %forward.1 = (bf16[1024,256]{1,0:T(8,128)(2,1)}, bf16[1152,256]{1,0:T(8,128)(2,1)}, bf16[1152,256]{1,0:T(8,128)(2,1)}, bf16[4,256,256]{2,1,0:T(8,128)(2,1)}, f32...) custom-call(bf16[256,1024]{1,0:T(8,128)(2,1)} %bitcast.17, ...), custom_call_target="tpu_custom_call" | custom-call | tf_op jit(solution)/shard_map/forward/pallas_call | solution.py:974
  99.9 26.6 %feed_forward.1 = (bf16[256,1024]{1,0:T(8,128)(2,1)}, f32[256,1024]{1,0:T(8,128)}, bf16[4,64,1024]{2,1,0:T(8,128)(2,1)}, bf16[2,64,1024]{2,1,0:T(8,128)(2,1)}, f32[8,1024]{1,0:T(8,128)}) custom-call(f32[256,1024]{1,0:T(8,128)} %get-tuple-element.50.v2, bf16[256,1024]{1,0:T(8,128)(2,1)} %bitcast.19, bf16[4,1024,1024]{2,1,0:T(8,128)(2,1)} %get-tuple-element.51.w_in, ...), custom_call_target="tpu_custom_call" | custom-call | tf_op jit(solution)/shard_map/feed_forward/pallas_call | solution.py:211
  126.5 68.1 %backward.1 = (bf16[256,1024]{1,0:T(8,128)(2,1)}, bf16[256,1024]{1,0:T(8,128)(2,1)}, bf16[2,2,4,64,1024]{4,3,2,1,0:T(8,128)(2,1)}, f32[64,256]{1,0:T(8,128)}, f32[96,256]{1,0:T(8,128)}) custom-call(f32[256,1024]{1,0:T(8,128)} %get-tuple-element.54.refs_0_, f32[256,1024]{1,0:T(8,128)} %get-tuple-element.55.refs_1_, ...), custom_call_target="tpu_custom_call" | custom-call | tf_op jit(solution)/shard_map/backward/pallas_call | solution.py:1327
  194.5 4.7 %finish.1 = (bf16[256,1024]{1,0:T(8,128)(2,1)}, bf16[256,1024]{1,0:T(8,128)(2,1)}, bf16[256,1024]{1,0:T(8,128)(2,1)}, f32[30,2,256]{2,1,0:T(2,128)}, f32[30,2,25...) custom-call(bf16[256,1024]{1,0:T(8,128)(2,1)} %get-tuple-element.53., ...), custom_call_target="tpu_custom_call" | custom-call | tf_op jit(solution)/shard_map/finish/pallas_call | solution.py:1440

commit v5 on v4

--- a/solution.py
+++ b/solution.py
@@ -876,8 +876,7 @@
 
     events = {
         0: [each(ffn.keep_own, late), each(ffn.along, (0, 1), 2)],
-        1: [each(ffn.came_over, (2,)), each(cross.complete, early)],
-        2: [each(ffn.came_over, (3,)), each(ffn.start_over, late, 1)],
+        1: [each(ffn.came_over, (2, 3)), each(cross.complete, early), each(ffn.start_over, late, 1)],
         3: [each(ffn.along, (2,), 0), each(cross.far_ready, early)],
         4: [each(ffn.along, (3,), 0), each(ffn.along, (2,), 1)],
         5: [each(ffn.along, (3,), 1)],
@@ -1135,7 +1134,7 @@
             dk[step, :, cols] = dk_pair[PRE:].astype(bf16)
             dv[step, :, cols] = dv_pair[PRE:].astype(bf16)
 
-            @pl.when((step == 1) & (j == 1))
+            @pl.when((step == 1) & (j == 0))
             def _():
                 reduce.start_line()
 

time: 200 us -> 199 us (level)
  no operation moved by 1% of the time
where the time goes in v5:
time: 199 us
  Pallas kernels  198 us (99%)
    pallas_call x1, Pallas kernels, forward(): pl.pallas_call(functools.partial(forward_kernel, prefix_len), grid=(1,),...  99.3 us
    pallas_call x1, Pallas kernels, backward(): pl.pallas_call(functools.partial(backward_kernel, prefix_len, reduce_leve...  67.6 us
    pallas_call x1, Pallas kernels, feed_forward(): pl.pallas_call(feed_forward_kernel, grid=(2 * n,), out_shape=outs, in_spe...  26.6 us
    pallas_call x1, Pallas kernels, finish(): pl.pallas_call(functools.partial(finish_kernel, prefix_len, lanes), grid=...  4.67 us

profile of v5, /device:TPU:0, one launch (start us, length us, event | category | flops | bytes accessed | tf_op | source)
XLA Modules:
  0.0 199.0 jit_solution(11557365304407528977)
XLA Ops:
  0.6 99.3 %forward.1 = (bf16[1024,256]{1,0:T(8,128)(2,1)}, bf16[1152,256]{1,0:T(8,128)(2,1)}, bf16[1152,256]{1,0:T(8,128)(2,1)}, bf16[4,256,256]{2,1,0:T(8,128)(2,1)}, f32...) custom-call(bf16[256,1024]{1,0:T(8,128)(2,1)} %bitcast.17, ...), custom_call_target="tpu_custom_call" | custom-call | tf_op jit(solution)/shard_map/forward/pallas_call | solution.py:973
  100.0 26.6 %feed_forward.1 = (bf16[256,1024]{1,0:T(8,128)(2,1)}, f32[256,1024]{1,0:T(8,128)}, bf16[4,64,1024]{2,1,0:T(8,128)(2,1)}, bf16[2,64,1024]{2,1,0:T(8,128)(2,1)}, f32[8,1024]{1,0:T(8,128)}) custom-call(f32[256,1024]{1,0:T(8,128)} %get-tuple-element.50.v2, bf16[256,1024]{1,0:T(8,128)(2,1)} %bitcast.19, bf16[4,1024,1024]{2,1,0:T(8,128)(2,1)} %get-tuple-element.51.w_in, ...), custom_call_target="tpu_custom_call" | custom-call | tf_op jit(solution)/shard_map/feed_forward/pallas_call | solution.py:211
  126.6 67.6 %backward.1 = (bf16[256,1024]{1,0:T(8,128)(2,1)}, bf16[256,1024]{1,0:T(8,128)(2,1)}, bf16[2,2,4,64,1024]{4,3,2,1,0:T(8,128)(2,1)}, f32[64,256]{1,0:T(8,128)}, f32[96,256]{1,0:T(8,128)}) custom-call(f32[256,1024]{1,0:T(8,128)} %get-tuple-element.54.refs_0_, f32[256,1024]{1,0:T(8,128)} %get-tuple-element.55.refs_1_, ...), custom_call_target="tpu_custom_call" | custom-call | tf_op jit(solution)/shard_map/backward/pallas_call | solution.py:1326
  194.2 4.7 %finish.1 = (bf16[256,1024]{1,0:T(8,128)(2,1)}, bf16[256,1024]{1,0:T(8,128)(2,1)}, bf16[256,1024]{1,0:T(8,128)(2,1)}, f32[30,2,256]{2,1,0:T(2,128)}, f32[30,2,25...) custom-call(bf16[256,1024]{1,0:T(8,128)(2,1)} %get-tuple-element.53., ...), custom_call_target="tpu_custom_call" | custom-call | tf_op jit(solution)/shard_map/finish/pallas_call | solution.py:1439
